TPU v7x, 32 devices: a whole 2x2x4 slice. The times are simulated.
32 devices in a mesh: chan: 4 (over y, x), win: 8 (over z, core).
Axes of the slice: x: 2, y: 2, z: 4, core: 2. Of those that a mesh axis runs over, the one named last changes fastest.
Arguments:
- traces: float32 [256, 16, 1024], P('chan', 'win'), may hold values from -80 to 80, as said below
- needed: int32 [4, 48], replicated, may hold values from 0 to 255, as said below
- home_slot: int32 [8, 8], P('chan'), may hold values from 0 to 47, as said below
- partner_slot: int32 [8, 16], P('chan'), may hold values from 0 to 47, as said below
- live_blocks: int32 [4], P('chan'), may hold values from 1 to 2, as said below
Outputs:
- correlations: float32 [1024, 1024], P(('chan', 'win'))
Inputs may be any that keep to these rules, and one draw needn't show every extreme that they name: `traces`: samples are bounded by the range. `needed`: each row lists 48 distinct channels in increasing order; row d holds exactly 24 channels of its own group d * 64 .. (d + 1) * 64 - 1 and at most 24 of any other group of 64 channels. `home_slot`: within one block the 8 home positions and 16 partner positions are all distinct. `partner_slot`: within one block the 8 home positions and 16 partner positions are all distinct. `live_blocks`: some owner uses all 2 slots and another owner uses only one.
All inputs are finite; a program needn't handle non-finite values.
Results may differ from a plain program's by a relative error of at most 0.0041.
Values may be sent and summed in bfloat16 or wider, within the bound.
A program may use at most 64 MiB of HBM per device.

v0:
```python
import math

import jax
import jax.numpy as jnp
from jax import lax
from jax.sharding import PartitionSpec as P

band_reach = 64


def forward_table(samples):
    freq_bins = samples // 2
    sample_index = jnp.arange(samples, dtype=jnp.int32)[:, None]
    freq_index = jnp.arange(freq_bins, dtype=jnp.int32)[None, :]
    phase_angle = (sample_index * freq_index % samples).astype(jnp.float32) * (
        2.0 * math.pi / samples
    )
    return jnp.concatenate([jnp.cos(phase_angle), -jnp.sin(phase_angle)], axis=1)


def inverse_table(samples):
    freq_bins = samples // 2
    freq_index = jnp.arange(freq_bins, dtype=jnp.int32)[:, None]
    lag_shift = (jnp.arange(samples, dtype=jnp.int32) - samples // 2) % samples
    phase_angle = (freq_index * lag_shift[None, :] % samples).astype(jnp.float32) * (
        2.0 * math.pi / samples
    )
    weight = jnp.where(freq_index == 0, 1.0, 2.0).astype(jnp.float32)
    return jnp.concatenate([weight * jnp.cos(phase_angle), -weight * jnp.sin(phase_angle)], axis=0)


def band_table(freq_bins):
    bin_index = jnp.arange(freq_bins, dtype=jnp.int32)
    inside = (jnp.abs(bin_index[:, None] - bin_index[None, :]) <= band_reach).astype(jnp.float32)
    return inside / jnp.sum(inside, axis=0, keepdims=True)


def whiten(trace_rows):
    samples = trace_rows.shape[-1]
    freq_bins = samples // 2
    spectrum = jnp.dot(trace_rows, forward_table(samples), precision=lax.Precision.HIGHEST)
    power_bins = spectrum[:, :freq_bins] ** 2 + spectrum[:, freq_bins:] ** 2
    smooth = jnp.dot(power_bins, band_table(freq_bins), precision=lax.Precision.HIGHEST)
    factor = 1.0 / jnp.sqrt(smooth + 1e-05)
    return (spectrum * jnp.concatenate([factor, factor], axis=1)).astype(jnp.bfloat16)


def pair_product(left_side, right_side):
    return jnp.einsum("bhwf,bpwf->bhpf", left_side, right_side, preferred_element_type=jnp.float32)


def cross_spectra(home_spectra, partners):
    freq_bins = home_spectra.shape[-1] // 2
    home_re, home_im = (home_spectra[..., :freq_bins], home_spectra[..., freq_bins:])
    part_re, part_im = (partners[..., :freq_bins], partners[..., freq_bins:])
    real_part = pair_product(home_re, part_re) + pair_product(home_im, part_im)
    imag_part = pair_product(home_im, part_re) - pair_product(home_re, part_im)
    joined = jnp.concatenate([real_part, imag_part], axis=-1)
    return joined.reshape(-1, joined.shape[-1])


def body(traces, needed, home_slot, partner_slot, live_blocks):
    chan_dev, win_dev, samples = traces.shape
    groups = lax.axis_size("chan")
    win_count = lax.axis_size("win")
    owner_index = lax.axis_index("chan")
    whitened = whiten(traces.reshape(chan_dev * win_dev, samples)).reshape(
        chan_dev, win_dev, samples
    )
    listed = lax.dynamic_index_in_dim(needed, owner_index, 0, keepdims=False)
    list_length = needed.shape[1]
    capacity = 2 * list_length // groups
    first_mine = owner_index * chan_dev
    begin_at = jnp.sum((needed < first_mine).astype(jnp.int32), axis=1)
    pick_at = jnp.minimum(
        begin_at[:, None] + jnp.arange(capacity, dtype=jnp.int32)[None, :], list_length - 1
    )
    chosen = jnp.take_along_axis(needed, pick_at, axis=1)
    local_rows = jnp.clip(chosen - first_mine, 0, chan_dev - 1)
    outgoing = whitened[local_rows]
    incoming = lax.all_to_all(outgoing, "chan", split_axis=0, concat_axis=0, tiled=True)
    source = listed // chan_dev
    group_index = jnp.arange(groups, dtype=jnp.int32)
    bounds = group_index * chan_dev
    start_at = jnp.sum((listed[None, :] < bounds[:, None]).astype(jnp.int32), axis=1)
    offset = jnp.sum(
        jnp.where(source[:, None] == group_index[None, :], start_at[None, :], 0), axis=1
    )
    position = source * capacity + jnp.arange(list_length, dtype=jnp.int32) - offset
    table_rows = incoming.reshape(groups * capacity, win_dev, samples)[position]
    inverse = inverse_table(samples)
    row_share = home_slot.shape[0] * home_slot.shape[1] * partner_slot.shape[1] // win_count
    cross_terms = cross_spectra(table_rows[home_slot], table_rows[partner_slot])
    correlated = lax.psum_scatter(
        jnp.dot(cross_terms, inverse, precision=lax.Precision.HIGHEST),
        "win",
        scatter_dimension=0,
        tiled=True,
    )
    norm_scale = 1.0 / math.sqrt(samples * win_dev * win_count)
    local_index = lax.axis_index("win") * row_share + jnp.arange(row_share, dtype=jnp.int32)
    block_index = local_index // (home_slot.shape[1] * partner_slot.shape[1])
    live_mask = (block_index < live_blocks[0]).astype(jnp.float32)
    return correlated * norm_scale * live_mask[:, None]


def solution(mesh):
    placed = (P("chan", "win", None), P(), P("chan", None), P("chan", None), P("chan"))
    return jax.shard_map(
        body, mesh=mesh, in_specs=placed, out_specs=P(("chan", "win"), None), check_vma=False
    )
```

profile of v0, /device:TPU:0, one launch (start us, length us, event | category | flops | bytes accessed | tf_op | source)
XLA Modules:
  0.0 113.0 jit_solution(11759462148276746869)
XLA Ops:
  6.5 9.1 %sine_negate_fusion = (f32[1024,512]{1,0:T(8,128)S(1)}, f32[1024,512]{1,0:T(8,128)}) fusion(), kind=kLoop, calls=%fused_computation.31 | loop fusion | flops 7864320 | bytes 4194304 | tf_op jit(solution)/shard_map/neg | solution.py:18
  15.6 0.1 convert_reduce_fusion
  15.8 0.1 convert_reduce_fusion.2
  16.0 0.1 reshape.315
  16.0 1.5 %gather_fusion.4 = s32[96]{0:T(128)S(1)} fusion(s32[4,48]{1,0:T(4,128)S(1)} %copy-done, s32[96]{0:T(128)S(1)} %reshape.315), kind=kCustom, calls=%fused_computation.4 | custom fusion | bytes 1536 | tf_op jit(solution)/shard_map/jit(take_along_axis)/gather | solution.py:78
  17.7 0.1 reshape.285
  17.8 0.4 reshape.279
  18.2 4.0 %fusion.20 = f32[128,1024]{1,0:T(8,128)S(1)} fusion(f32[128,1024]{1,0:T(8,128)S(1)} %reshape.279, f32[1024,512]{1,0:T(8,128)S(1)} %get-tuple-element.13, f32[1024,512]{1,0:T(8,128)} %get-tuple-element.14), kind=kOutput, calls=%fused_computation.38 | convolution fusion | flops 1611661312 | bytes 5242880 | tf_op jit(solution)/shard_map/dot_general | solution.py:41
  22.2 0.7 fusion.23
  23.0 0.1 reshape.280
  23.2 2.2 %gather_fusion = bf16[96,2,1024]{2,1,0:T(2,128)(2,1)} fusion(bf16[64,2,1024]{2,1,0:T(2,128)(2,1)S(1)} %reshape.280, s32[1024]{0:T(1024)S(1)} %pad_clamp_fusion.3), kind=kCustom, calls=%fused_computation | custom fusion | bytes 786816 | tf_op jit(solution)/shard_map/gather | solution.py:80
  25.3 5.2 %all-to-all-start = ((bf16[4,24,2,1024]{3,2,1,0:T(2,128)(2,1)}), bf16[4,24,2,1024]{3,2,1,0:T(2,128)(2,1)S(1)}, u32[]{:S(2)}, u32[]{:S(2)}) async-start(bf16[4,24,2,1024]{3,2,1,0:T(2,128)(2,1)} %bitcast.1), calls=%async_computation | async-start | bytes 786432 | tf_op jit(solution)/shard_map/all_to_all | solution.py:81
  30.5 0.2 convert_reduce_fusion.1
  30.7 0.1 select_reduce_fusion
  31.1 9.2 %cosine_multiply_fusion = (f32[512,1024]{1,0:T(8,128)S(1)}, f32[512,1024]{1,0:T(8,128)}) fusion(s32[1024]{0:T(1024)S(1)} %add_select_fusion.2, f32[512]{0:T(512)S(1)} %get-tuple-element.15, f32[512]{0:T(512)S(1)} %get-tuple-element.16), kind=kLoop, calls=%fused_computation.28 | loop fusion | flops 8388608 | bytes 4202496 | tf_op jit(solution)/shard_map/mul | solution.py:29
  40.2 1.0 gather_fusion.1
  41.2 0.8 gather_fusion.2
  42.1 0.4 copy.34
  42.5 0.7 gather_fusion.3
  43.2 0.4 copy.35
  43.6 1.1 copy.36
  44.7 1.1 copy.37
  45.7 1.4 %fusion.44 = f32[2,512,16,8]{2,3,1,0:T(8,128)S(1)} fusion(bf16[2,16,2,512]{1,2,3,0:T(2,128)(2,1)S(1)} %copy.34, bf16[2,8,2,512]{1,2,3,0:T(2,128)(2,1)S(1)} %copy.35), kind=kOutput, calls=%fused_computation.101 | convolution fusion | flops 524288 | bytes 622592 | tf_op jit(solution)/shard_map/bhwf,bpwf->bhpf/dot_general | solution.py:49
  47.2 2.9 %fusion.45 = f32[2,512,16,8]{2,3,1,0:T(8,128)} fusion(bf16[2,16,2,512]{1,2,3,0:T(2,128)(2,1)S(1)} %copy.34, bf16[2,8,2,512]{1,2,3,0:T(2,128)(2,1)S(1)} %copy-done.4), kind=kOutput, calls=%fused_computation.102 | convolution fusion | flops 524288 | bytes 622592 | tf_op jit(solution)/shard_map/bhwf,bpwf->bhpf/dot_general | solution.py:49
  50.1 3.0 %add_bitcast_fusion = f32[2,8,16,512]{2,1,3,0:T(8,128)} fusion(f32[2,512,16,8]{2,3,1,0:T(8,128)S(1)} %fusion.44, bf16[2,16,2,512]{1,2,3,0:T(2,128)(2,1)S(1)} %copy-done.2, bf16[2,8,2,512]{1,2,3,0:T(2,128)(2,1)S(1)} %copy-done.4), kind=kOutput, calls=%fused_computation.14 | convolution fusion | flops 655360 | bytes 1146880 | tf_op jit(solution)/shard_map/bhwf,bpwf->bhpf/dot_general | solution.py:49
  53.1 3.6 %copy.32 = f32[2,8,16,512]{3,2,1,0:T(8,128)} copy(f32[2,8,16,512]{2,1,3,0:T(8,128)} %add_bitcast_fusion) | data formatting | bytes 1048576 | tf_op jit(solution)/shard_map/add | solution.py:56
  56.7 4.5 %subtract_bitcast_fusion = f32[2,8,16,512]{2,1,3,0:T(8,128)} fusion(f32[2,512,16,8]{2,3,1,0:T(8,128)} %fusion.45, bf16[2,16,2,512]{1,2,3,0:T(2,128)(2,1)S(1)} %copy-done.3, bf16[2,8,2,512]{1,2,3,0:T(2,128)(2,1)S(1)} %copy.35), kind=kOutput, calls=%fused_computation.13 | convolution fusion | flops 655360 | bytes 1146880 | tf_op jit(solution)/shard_map/bhwf,bpwf->bhpf/dot_general | solution.py:49
  61.2 2.8 %copy.33 = f32[2,8,16,512]{3,2,1,0:T(8,128)S(1)} copy(f32[2,8,16,512]{2,1,3,0:T(8,128)} %subtract_bitcast_fusion) | data formatting | bytes 1048576 | tf_op jit(solution)/shard_map/sub | solution.py:57
  64.1 1.5 %copy-done.1 = f32[512,1024]{1,0:T(8,128)S(1)} copy-done((f32[512,1024]{1,0:T(8,128)S(1)}, f32[512,1024]{1,0:T(8,128)}, u32[]{:S(2)}) %copy-start.1) | copy-done | bytes 2097176
  65.6 4.7 %fusion.4 = f32[256,1024]{1,0:T(8,128)} fusion(f32[256,1024]{1,0:T(8,128)S(1)} %bitcast.48, f32[512,1024]{1,0:T(8,128)S(1)} %copy-done.1, f32[512,1024]{1,0:T(8,128)S(1)} %get-tuple-element.11), kind=kOutput, calls=%fused_computation.9 | convolution fusion | flops 3222274048 | bytes 6291456 | tf_op jit(solution)/shard_map/dot_general | solution.py:95
  71.0 33.5 %reduce-scatter.2.cloned.1.call-done = f32[32,1024]{1,0:T(8,128)} async-done(((f32[256,1024]{1,0:T(8,128)}), f32[32,1024]{1,0:T(8,128)}) %reduce-scatter.2.cloned.1.call-update) | async-done | bytes 131088 | tf_op jit(solution)/shard_map/reduce_scatter | solution.py:94
  104.5 1.6 %broadcast_multiply_fusion = f32[32,1024]{1,0:T(8,128)} fusion(f32[32,1024]{1,0:T(8,128)} %reduce-scatter.2.cloned.1.call-done, f32[32]{0:T(128)S(1)} %compare_select_fusion.5), kind=kLoop, calls=%fused_computation.52 | loop fusion | flops 32768 | bytes 262272 | tf_op jit(solution)/shard_map/mul | solution.py:104
  (43 shorter events, 0.8 us)
Async XLA Ops:
  6.5 9.2 %copy-start = (s32[4,48]{1,0:T(4,128)S(1)}, s32[4,48]{1,0:T(4,128)}, u32[]{:S(2)}) copy-start(s32[4,48]{1,0:T(4,128)} %param.6) | copy-start | bytes 2308
  15.6 2.2 %copy-start.6 = (f32[64,2,1024]{2,1,0:T(2,128)S(1)}, f32[64,2,1024]{2,1,0:T(2,128)}, u32[]{:S(2)}) copy-start(f32[64,2,1024]{2,1,0:T(2,128)} %param.5) | copy-start | bytes 1572868
  22.9 7.9 %copy-start.7 = (s32[2,16]{1,0:T(2,128)S(1)}, s32[2,16]{1,0:T(2,128)}, u32[]{:S(2)}) copy-start(s32[2,16]{1,0:T(2,128)} %param.8) | copy-start | bytes 388
  23.0 8.0 %copy-start.8 = (s32[2,8]{1,0:T(2,128)S(1)}, s32[2,8]{1,0:T(2,128)}, u32[]{:S(2)}) copy-start(s32[2,8]{1,0:T(2,128)} %param.7) | copy-start | bytes 196
  25.3 14.9 %all-to-all-start = ((bf16[4,24,2,1024]{3,2,1,0:T(2,128)(2,1)}), bf16[4,24,2,1024]{3,2,1,0:T(2,128)(2,1)S(1)}, u32[]{:S(2)}, u32[]{:S(2)}) async-start(bf16[4,24,2,1024]{3,2,1,0:T(2,128)(2,1)} %bitcast.1), calls=%async_computation | async-start | bytes 786432 | tf_op jit(solution)/shard_map/all_to_all | solution.py:81
  30.5 74.1 %reduce-scatter.2.cloned.1.call-start = ((), (), s32[]{:S(2)}) async-start(), calls=%async_computation.2 | async-start | bytes 1179648 | tf_op jit(solution)/shard_map/reduce_scatter | solution.py:94
  45.7 1.4 %copy-start.4 = (bf16[2,8,2,512]{1,2,3,0:T(2,128)(2,1)S(1)}, bf16[2,8,2,512]{1,2,3,0:T(2,128)(2,1)}, u32[]{:S(2)}) copy-start(bf16[2,8,2,512]{1,2,3,0:T(2,128)(2,1)} %copy.37) | copy-start | bytes 98308
  47.1 3.0 %copy-start.2 = (bf16[2,16,2,512]{1,2,3,0:T(2,128)(2,1)S(1)}, bf16[2,16,2,512]{1,2,3,0:T(2,128)(2,1)}, u32[]{:S(2)}) copy-start(bf16[2,16,2,512]{1,2,3,0:T(2,128)(2,1)} %copy.36) | copy-start | bytes 196612
  53.1 3.6 %copy-start.3 = (bf16[2,16,2,512]{1,2,3,0:T(2,128)(2,1)S(1)}, bf16[2,16,2,512]{1,2,3,0:T(2,128)(2,1)}, u32[]{:S(2)}) copy-start(bf16[2,16,2,512]{1,2,3,0:T(2,128)(2,1)} %copy.36) | copy-start | bytes 196612
  61.2 2.9 %copy-start.5 = (f32[2,8,16,512]{3,2,1,0:T(8,128)S(1)}, f32[2,8,16,512]{3,2,1,0:T(8,128)}, u32[]{:S(2)}) copy-start(f32[2,8,16,512]{3,2,1,0:T(8,128)} %copy.32) | copy-start | bytes 1572868
  64.0 1.6 %copy-start.1 = (f32[512,1024]{1,0:T(8,128)S(1)}, f32[512,1024]{1,0:T(8,128)}, u32[]{:S(2)}) copy-start(f32[512,1024]{1,0:T(8,128)} %get-tuple-element.12) | copy-start | bytes 6291460
Sparse Core Ops, SparseCore 0:
  70.5 34.0 reduce-scatter.1
where the time goes:
time: 113 us
  waiting for transfers between devices  33.6 us (30%)
  matrix products  21.3 us (19%)
  other arithmetic  20.8 us (18%)
  local copies, waits for them, and re-layouts  17.9 us (16%)
  between operations  14.3 us (13%)
  starting transfers between devices  5.17 us (5%)
    reduce_scatter x1, waiting for transfers between devices, body(): lax.psum_scatter(jnp.dot(cross_terms, inverse, precision=lax.Precision.HI...  33.5 us
    dot_general x4, matrix products, pair_product(): jnp.einsum('bhwf,bpwf->bhpf', left_side, right_side, preferred_element_ty...  11.9 us
    mul x1, other arithmetic, inverse_table(): weight * jnp.cos(phase_angle)  9.17 us
    neg x1, other arithmetic, forward_table(): -jnp.sin(phase_angle)  9.09 us
    all_to_all x1, starting transfers between devices, body(): lax.all_to_all(outgoing, 'chan', split_axis=0, concat_axis=0, tiled=True)  5.17 us
    dot_general x1, matrix products, body(): jnp.dot(cross_terms, inverse, precision=lax.Precision.HIGHEST)  4.68 us
    unnamed x22, local copies, waits for them, and re-layouts  4.44 us
    dot_general x1, matrix products, whiten(): jnp.dot(trace_rows, forward_table(samples), precision=lax.Precision.HIGHEST)  4.01 us
  transfers between devices with their start and end apart: 2, of which 1 were waited for; matrix products, arithmetic and copies ran while one was open for 9% of the time, Pallas kernels for 0%

commit v1 on v0

v1 whole, which is shorter than its diff:
```python
import functools
import math

import jax
import jax.numpy as jnp
import ml_dtypes
import numpy as np
from jax import lax
from jax.experimental import pallas as pl
from jax.experimental.pallas import tpu as pltpu
from jax.sharding import PartitionSpec as P

MESH = pl.DeviceIdType.MESH
BAND_REACH = 64
CHUNKS = 4


def split_table(table):
    high = table.astype(np.float32).astype(ml_dtypes.bfloat16)
    low = (table - high.astype(np.float64)).astype(np.float32).astype(ml_dtypes.bfloat16)
    return high, low


@functools.lru_cache(maxsize=None)
def tables(samples):
    quarter, half = samples // 4, samples // 2
    eighth = samples // 8
    bins_a = np.arange(0, half, 4)
    bins_b = np.arange(2, half, 4)
    bins_o = np.arange(1, half, 2)

    def forward(length, bins):
        phase = (np.arange(length)[:, None] * bins[None, :] % samples) * (2.0 * np.pi / samples)
        return np.cos(phase), -np.sin(phase)

    def inverse(length, bins):
        phase = (bins[:, None] * np.arange(length)[None, :] % samples) * (2.0 * np.pi / samples)
        weight = np.where(bins == 0, 1.0, 2.0)[:, None]
        return weight * np.cos(phase), -weight * np.sin(phase)

    odd_cos, odd_sin = forward(half, bins_o)
    fwd_a = np.concatenate(forward(quarter, bins_a), axis=1)
    fwd_b = np.concatenate(forward(quarter, bins_b), axis=1)
    fwd_o = np.concatenate(
        [odd_cos[:, :eighth], odd_sin[:, :eighth], odd_cos[:, eighth:], odd_sin[:, eighth:]], axis=1
    )
    fwd_even = np.stack([x for t in (fwd_a, fwd_b) for x in split_table(t)])
    fwd_odd = np.stack(split_table(fwd_o))
    order = np.concatenate([bins_a, bins_b, bins_o])
    inside = np.abs(order[:, None] - order[None, :]) <= BAND_REACH
    band = inside.astype(np.float32).astype(ml_dtypes.bfloat16)
    share = (1.0 / inside.sum(axis=0, keepdims=True)).astype(np.float32)
    inv_cos, inv_sin = inverse(half, bins_o)
    inv_even = np.stack(
        [
            split_table(np.concatenate(inverse(quarter, bins), axis=0))[0]
            for bins in (bins_a, bins_b)
        ]
    )
    inv_odd = np.stack(
        [
            split_table(np.concatenate([inv_cos[rows], inv_sin[rows]], axis=0))[0]
            for rows in (slice(0, eighth), slice(eighth, None))
        ]
    )
    return fwd_even, fwd_odd, band, share, inv_even, inv_odd


def dot(left, right):
    return jnp.dot(left, right, preferred_element_type=jnp.float32)


def halves(value):
    high = value.astype(jnp.bfloat16)
    low = (value - high.astype(jnp.float32)).astype(jnp.bfloat16)
    return high, low


def as_column(row):
    n = row.shape[1]
    eye = lax.broadcasted_iota(jnp.int32, (n, n), 0) == lax.broadcasted_iota(jnp.int32, (n, n), 1)
    return jnp.sum(jnp.where(eye, jnp.broadcast_to(row, (n, n)), 0), axis=1, keepdims=True)


def kernel(
    dims,
    traces_hbm,
    needed_ref,
    home_ref,
    partner_ref,
    live_ref,
    fwd_even_hbm,
    fwd_odd_hbm,
    band_hbm,
    share_ref,
    inv_even_hbm,
    inv_odd_hbm,
    out_ref,
    traces,
    fwd_even,
    fwd_odd,
    band,
    inv_even,
    inv_odd,
    listed_out,
    listed_in,
    terms,
    terms_out,
    pair_in,
    chip_sum,
    chip_out,
    chip_in,
    load_sem,
    list_send,
    list_recv,
    pair_send,
    pair_recv,
    chip_send,
    chip_recv,
):
    groups, win_count, chan_dev, win_dev, samples, listing, cap, cap_rows, blocks, homes, partners = dims
    chips = win_count // 2
    pairs = blocks * homes * partners
    share_rows = pairs // win_count
    pad_rows = terms.shape[2] // chips
    quarter, half, eighth = samples // 4, samples // 2, samples // 8
    group = lax.axis_index("chan")
    win = lax.axis_index("win")
    chip, core = win // 2, win % 2

    loads = [
        pltpu.make_async_copy(src, dst, load_sem.at[i])
        for i, (src, dst) in enumerate(
            (
                (traces_hbm, traces),
                (fwd_even_hbm, fwd_even),
                (fwd_odd_hbm, fwd_odd),
                (band_hbm, band),
                (inv_even_hbm, inv_even),
                (inv_odd_hbm, inv_odd),
            )
        )
    ]
    for load in loads:
        load.start()

    barrier = pltpu.get_barrier_semaphore()
    group_peers = [lax.rem(group + d, groups) for d in range(1, groups)]
    chip_peers = [lax.rem(chip + d, chips) for d in range(1, chips)]
    for peer in group_peers:
        pl.semaphore_signal(barrier, inc=1, device_id={"chan": peer}, device_id_type=MESH)
    pl.semaphore_signal(
        barrier, inc=1, device_id={"win": chip * 2 + 1 - core}, device_id_type=MESH
    )
    for peer in chip_peers:
        pl.semaphore_signal(
            barrier, inc=1, device_id={"win": peer * 2 + core}, device_id_type=MESH
        )

    lanes = win_dev * chan_dev
    lane = lax.broadcasted_iota(jnp.int32, (1, lanes), 1)
    lane_win = sum([(lane >= w * chan_dev).astype(jnp.int32) for w in range(1, win_dev)])
    lane_chan = lane - lane_win * chan_dev
    first_mine = group * chan_dev
    place = lax.broadcasted_iota(jnp.int32, (listing, lanes), 0)
    out_row = lax.broadcasted_iota(jnp.int32, (cap_rows, lanes), 0)
    choose = []
    for d in range(groups):
        owner = lax.rem(group + d, groups)
        column = as_column(needed_ref[pl.ds(owner, 1), :])
        hit = column == (lane_chan + first_mine)
        found = jnp.sum(jnp.where(hit, place + 1, 0), axis=0, keepdims=True)
        begin = jnp.sum((column < first_mine).astype(jnp.int32), axis=0, keepdims=True)
        target = jnp.where(found > 0, found - 1 - begin + lane_win * cap, -1)
        choose.append(jnp.where(out_row == target, 1.0, 0.0))
    choose = jnp.concatenate(choose, axis=0).astype(jnp.bfloat16)

    mine = needed_ref[pl.ds(group, 1), :]
    arrived = lax.broadcasted_iota(jnp.int32, (1, groups * cap_rows), 1)
    code = jnp.full((1, groups * cap_rows), -1, jnp.int32)
    for d in range(groups):
        source = lax.rem(group + groups - d, groups)
        begin = jnp.sum(
            (mine < source * chan_dev).astype(jnp.int32), axis=1, keepdims=True
        )
        for w in range(win_dev):
            low = d * cap_rows + w * cap
            within = (arrived >= low) & (arrived < low + cap)
            code = jnp.where(within, arrived - low + begin + w * listing, code)
    wanted = [as_column(partner_ref[b : b + 1, :]) for b in range(blocks)]
    wanted += [as_column(home_ref[b : b + 1, :]) for b in range(blocks)]
    wanted = jnp.concatenate(wanted, axis=0)
    per_win = blocks * (homes + partners)
    wanted = jnp.concatenate([wanted + w * listing for w in range(win_dev)], axis=0)
    pick = jnp.where(wanted == code, 1.0, 0.0).astype(jnp.bfloat16)

    loads[0].wait()
    rows = jnp.concatenate([traces[:, w, :] for w in range(win_dev)], axis=0)
    count = rows.shape[0]
    folded = rows[:, :half] + rows[:, half:]
    odd_in = rows[:, :half] - rows[:, half:]
    even_in = (folded[:, :quarter] + folded[:, quarter:], folded[:, :quarter] - folded[:, quarter:])

    def transform(value, high_table, low_table):
        high, low = halves(value)
        both = dot(jnp.concatenate([high, low], axis=0), high_table)
        return both[:count] + both[count:] + dot(high, low_table)

    loads[1].wait()
    spectra = [
        transform(even_in[0], fwd_even[0], fwd_even[1]),
        transform(even_in[1], fwd_even[2], fwd_even[3]),
    ]
    loads[2].wait()
    odd_out = transform(odd_in, fwd_odd[0], fwd_odd[1])
    spectra += [odd_out[:, :quarter], odd_out[:, quarter:]]
    power = jnp.concatenate([s[:, :eighth] ** 2 + s[:, eighth:] ** 2 for s in spectra], axis=1)
    loads[3].wait()
    both = dot(jnp.concatenate(halves(power), axis=0), band[...])
    smooth = (both[:count] + both[count:]) * share_ref[...]
    factor = 1.0 / jnp.sqrt(smooth + 1e-05)

    pl.semaphore_wait(barrier, (groups - 1) + 1 + (chips - 1))

    list_copies = []
    for k in range(CHUNKS):
        scale = factor[:, k * eighth : (k + 1) * eighth]
        whitened = jnp.concatenate(
            [spectra[k][:, :eighth] * scale, spectra[k][:, eighth:] * scale], axis=1
        ).astype(jnp.bfloat16)
        chosen = dot(choose, whitened).astype(jnp.bfloat16)
        listed_in[k, 0] = chosen[:cap_rows]
        copies = []
        for d in range(1, groups):
            listed_out[k, d - 1] = chosen[d * cap_rows : (d + 1) * cap_rows]
            copies.append(
                pltpu.make_async_remote_copy(
                    src_ref=listed_out.at[k, d - 1],
                    dst_ref=listed_in.at[k, d],
                    send_sem=list_send.at[k, d - 1],
                    recv_sem=list_recv.at[k, d - 1],
                    device_id={"chan": group_peers[d - 1]},
                    device_id_type=MESH,
                )
            )
            copies[-1].start()
        list_copies.append(copies)

    pair_copies = [
        pltpu.make_async_remote_copy(
            src_ref=terms_out.at[k, 1 - core],
            dst_ref=pair_in.at[k],
            send_sem=pair_send.at[k],
            recv_sem=pair_recv.at[k],
            device_id={"win": chip * 2 + 1 - core},
            device_id_type=MESH,
        )
        for k in range(CHUNKS)
    ]
    chip_copies = [
        [
            pltpu.make_async_remote_copy(
                src_ref=chip_out.at[k, chip_peers[d - 1]],
                dst_ref=chip_in.at[k, d - 1],
                send_sem=chip_send.at[k, d - 1],
                recv_sem=chip_recv.at[k, d - 1],
                device_id={"win": chip_peers[d - 1] * 2 + core},
                device_id_type=MESH,
            )
            for d in range(1, chips)
        ]
        for k in range(CHUNKS)
    ]

    def cross(k):
        for copy in list_copies[k]:
            copy.wait_recv()
        table = dot(pick, listed_in[k].reshape(groups * cap_rows, quarter))
        piece = min(partners, share_rows)
        for b in range(blocks):
            for i in range(homes):
                real = imag = None
                for w in range(win_dev):
                    at = w * per_win + blocks * partners + b * homes + i
                    home_re = table[at : at + 1, :eighth]
                    home_im = table[at : at + 1, eighth:]
                    at = w * per_win + b * partners
                    part_re = table[at : at + partners, :eighth]
                    part_im = table[at : at + partners, eighth:]
                    add_re = home_re * part_re + home_im * part_im
                    add_im = home_im * part_re - home_re * part_im
                    real = add_re if real is None else real + add_re
                    imag = add_im if imag is None else imag + add_im
                term = jnp.concatenate([real, imag], axis=1)
                for j in range(0, partners, piece):
                    row = (b * homes + i) * partners + j
                    owner, inner = row // share_rows, row % share_rows
                    at = (owner // 2) * pad_rows + inner
                    terms[k, owner % 2, at : at + piece, :] = term[j : j + piece]
        terms_out[k, 1 - core] = terms[k, 1 - core].astype(jnp.bfloat16)
        pair_copies[k].start()

    def across(k):
        pair_copies[k].wait_recv()
        total = terms[k, core] + pair_in[k].astype(jnp.float32)
        total = total.reshape(chips, pad_rows, quarter)
        chip_sum[k] = total
        chip_out[k] = total.astype(jnp.bfloat16)
        for copy in chip_copies[k]:
            copy.start()

    for k in range(CHUNKS):
        cross(k)
        if k:
            across(k - 1)
    across(CHUNKS - 1)

    loads[4].wait()
    loads[5].wait()
    parts = []
    for k in range(CHUNKS):
        for copy in chip_copies[k]:
            copy.wait_recv()
        total = chip_sum[k, chip]
        for d in range(1, chips):
            total = total + chip_in[k, d - 1].astype(jnp.float32)
        table = inv_even[k] if k < 2 else inv_odd[k - 2]
        both = dot(jnp.concatenate(halves(total), axis=0), table)
        parts.append(both[:pad_rows] + both[pad_rows:])
    even = jnp.concatenate([parts[0] + parts[1], parts[0] - parts[1]], axis=1)
    odd = parts[2] + parts[3]
    norm = 1.0 / math.sqrt(samples * win_dev * win_count)
    row = win * share_rows + lax.broadcasted_iota(jnp.int32, (pad_rows, 1), 0)
    block = sum([(row >= b * homes * partners).astype(jnp.int32) for b in range(1, blocks)])
    gain = jnp.where(block < live_ref[0], norm, 0.0)
    out_ref[:, :half] = ((even - odd) * gain)[:share_rows]
    out_ref[:, half:] = ((even + odd) * gain)[:share_rows]

    for k in range(CHUNKS):
        for copy in list_copies[k] + [pair_copies[k]] + chip_copies[k]:
            copy.wait_send()


def body(traces, needed, home_slot, partner_slot, live_blocks):
    chan_dev, win_dev, samples = traces.shape
    groups, win_count = lax.axis_size("chan"), lax.axis_size("win")
    listing = needed.shape[1]
    cap = 2 * listing // groups
    cap_rows = -(-win_dev * cap // 16) * 16
    blocks, homes = home_slot.shape
    partners = partner_slot.shape[1]
    chips = win_count // 2
    share_rows = blocks * homes * partners // win_count
    pad_rows = max(share_rows, 16)
    quarter = samples // 4
    fwd_even, fwd_odd, band, share, inv_even, inv_odd = tables(samples)
    dims = (groups, win_count, chan_dev, win_dev, samples, listing, cap, cap_rows, blocks, homes, partners)
    vmem = pl.BlockSpec(memory_space=pltpu.VMEM)
    smem = pl.BlockSpec(memory_space=pltpu.SMEM)
    hbm = pl.BlockSpec(memory_space=pl.ANY)
    bf16, f32 = jnp.bfloat16, jnp.float32
    return pl.pallas_call(
        functools.partial(kernel, dims),
        out_shape=jax.ShapeDtypeStruct((share_rows, samples), f32),
        in_specs=[hbm, vmem, vmem, vmem, smem, hbm, hbm, hbm, vmem, hbm, hbm],
        out_specs=vmem,
        scratch_shapes=[
            pltpu.VMEM(traces.shape, f32),
            pltpu.VMEM(fwd_even.shape, bf16),
            pltpu.VMEM(fwd_odd.shape, bf16),
            pltpu.VMEM(band.shape, bf16),
            pltpu.VMEM(inv_even.shape, bf16),
            pltpu.VMEM(inv_odd.shape, bf16),
            pltpu.VMEM((CHUNKS, groups - 1, cap_rows, quarter), bf16),
            pltpu.VMEM((CHUNKS, groups, cap_rows, quarter), bf16),
            pltpu.VMEM((CHUNKS, 2, chips * pad_rows, quarter), f32),
            pltpu.VMEM((CHUNKS, 2, chips * pad_rows, quarter), bf16),
            pltpu.VMEM((CHUNKS, chips * pad_rows, quarter), bf16),
            pltpu.VMEM((CHUNKS, chips, pad_rows, quarter), f32),
            pltpu.VMEM((CHUNKS, chips, pad_rows, quarter), bf16),
            pltpu.VMEM((CHUNKS, chips - 1, pad_rows, quarter), bf16),
            pltpu.SemaphoreType.DMA((6,)),
            pltpu.SemaphoreType.DMA((CHUNKS, groups - 1)),
            pltpu.SemaphoreType.DMA((CHUNKS, groups - 1)),
            pltpu.SemaphoreType.DMA((CHUNKS,)),
            pltpu.SemaphoreType.DMA((CHUNKS,)),
            pltpu.SemaphoreType.DMA((CHUNKS, chips - 1)),
            pltpu.SemaphoreType.DMA((CHUNKS, chips - 1)),
        ],
        compiler_params=pltpu.CompilerParams(
            collective_id=0, has_side_effects=True, vmem_limit_bytes=40 * 1024 * 1024
        ),
        cost_estimate=pl.CostEstimate(
            flops=2_000_000_000, bytes_accessed=4_000_000, transcendentals=100_000
        ),
        name="whiten_cross_stack",
    )(
        traces,
        needed,
        home_slot,
        partner_slot,
        live_blocks,
        jnp.asarray(fwd_even),
        jnp.asarray(fwd_odd),
        jnp.asarray(band),
        jnp.asarray(share),
        jnp.asarray(inv_even),
        jnp.asarray(inv_odd),
    )


def solution(mesh):
    placed = (P("chan", "win", None), P(), P("chan", None), P("chan", None), P("chan"))
    return jax.shard_map(
        body, mesh=mesh, in_specs=placed, out_specs=P(("chan", "win"), None), check_vma=False
    )
```

time: 113 us -> 28.8 us (0.25)
  waiting for transfers between devices: 33.6 us -> 0 us
  matrix products: 21.3 us -> 0 us
  other arithmetic: 20.8 us -> 0 us
  Pallas kernels: 0 us -> 19.3 us
  between operations: 14.3 us -> 0.72 us
  local copies, waits for them, and re-layouts: 17.9 us -> 8.36 us
  starting transfers between devices: 5.17 us -> 0 us
    reduce_scatter x1 -> x0, waiting for transfers between devices: 33.5 us -> none  [body(): lax.psum_scatter(jnp.dot(cross_terms, inverse, precision=lax.Precision.HI...]
    dot_general x7 -> x0, matrix products: 21.3 us -> none  [the longest x4 11.9 us: pair_product(): jnp.einsum('bhwf,bpwf->bhpf', left_side, right_side, preferred_element_ty...]
    pallas_call x0 -> x1, Pallas kernels: none -> 19.3 us  [body(): pl.pallas_call(functools.partial(kernel, dims), out_shape=jax.ShapeDtypeS...]
    mul x4 -> x0, other arithmetic: 10.8 us -> none  [the longest x1 9.17 us: inverse_table(): weight * jnp.cos(phase_angle)]
    neg x1 -> x0, other arithmetic: 9.09 us -> none  [forward_table(): -jnp.sin(phase_angle)]
    gather x9 -> x0, local copies, waits for them, and re-layouts: 6.35 us -> none  [the longest x1 2.16 us: body(): outgoing = whitened[local_rows]]
    all_to_all x1 -> x0, starting transfers between devices: 5.17 us -> none  [body(): lax.all_to_all(outgoing, 'chan', split_axis=0, concat_axis=0, tiled=True)]
    unnamed x22 -> x21, local copies, waits for them, and re-layouts: 4.44 us -> 8.36 us
  transfers between devices with their start and end apart: 2 -> 0, of which waited for: 1 -> 0; matrix products, arithmetic and copies ran while one was open for 9% -> 0% of each run, Pallas kernels for 0% -> 0%
where the time goes in v1:
time: 28.8 us; the launch traced here: 28.3 us
  Pallas kernels  19.3 us (67%)
  local copies, waits for them, and re-layouts  8.36 us (29%)
  between operations  0.72 us (2%)
    pallas_call x1, Pallas kernels, body(): pl.pallas_call(functools.partial(kernel, dims), out_shape=jax.ShapeDtypeS...  19.3 us
    unnamed x21, local copies, waits for them, and re-layouts  8.36 us

profile of v1, /device:TPU:0, one launch (start us, length us, event | category | flops | bytes accessed | tf_op | source)
XLA Modules:
  0.0 28.3 jit_solution(14313071714361960496)
XLA Ops:
  0.0 0.0 copy-start.9
  0.0 0.0 copy-start.2
  0.7 0.0 copy-done.9
  0.7 0.0 copy-done.2
  0.7 0.0 copy-start
  0.7 1.0 %copy-done = f32[64,2,1024]{2,1,0:T(2,128)S(1)} copy-done((f32[64,2,1024]{2,1,0:T(2,128)S(1)}, f32[64,2,1024]{2,1,0:T(2,128)}, u32[]{:S(2)}) %copy-start) | copy-done | bytes 524312
  1.7 0.0 copy-start.1
  1.7 0.7 %copy-done.1 = s32[4,48]{1,0:T(4,128)S(1)} copy-done((s32[4,48]{1,0:T(4,128)S(1)}, s32[4,48]{1,0:T(4,128)}, u32[]{:S(2)}) %copy-start.1) | copy-done | bytes 792
  2.4 0.0 copy-start.3
  2.4 0.7 %copy-done.3 = s32[2,16]{1,0:T(2,128)S(1)} copy-done((s32[2,16]{1,0:T(2,128)S(1)}, s32[2,16]{1,0:T(2,128)}, u32[]{:S(2)}) %copy-start.3) | copy-done | bytes 152
  3.1 0.0 copy-start.4
  3.1 1.2 %copy-done.4 = bf16[2,512,512]{2,1,0:T(8,128)(2,1)S(1)} copy-done((bf16[2,512,512]{2,1,0:T(8,128)(2,1)S(1)}, bf16[2,512,512]{2,1,0:T(8,128)(2,1)}, u32[]{:S(2)}) %copy-start.4) | copy-done | bytes 1048600
  4.3 0.0 copy-start.5
  4.3 1.0 %copy-done.5 = bf16[2,256,512]{2,1,0:T(8,128)(2,1)S(1)} copy-done((bf16[2,256,512]{2,1,0:T(8,128)(2,1)S(1)}, bf16[2,256,512]{2,1,0:T(8,128)(2,1)}, u32[]{:S(2)}) %copy-start.5) | copy-done | bytes 524312
  5.4 0.0 copy-start.6
  5.4 1.0 %copy-done.6 = bf16[512,512]{1,0:T(8,128)(2,1)S(1)} copy-done((bf16[512,512]{1,0:T(8,128)(2,1)S(1)}, bf16[512,512]{1,0:T(8,128)(2,1)}, u32[]{:S(2)}) %copy-start.6) | copy-done | bytes 524312
  6.4 0.0 copy-start.7
  6.4 1.0 %copy-done.7 = bf16[4,256,256]{2,1,0:T(8,128)(2,1)S(1)} copy-done((bf16[4,256,256]{2,1,0:T(8,128)(2,1)S(1)}, bf16[4,256,256]{2,1,0:T(8,128)(2,1)}, u32[]{:S(2)}) %copy-start.7) | copy-done | bytes 524312
  7.5 0.0 copy-start.8
  7.5 0.9 %copy-done.8 = bf16[2,256,256]{2,1,0:T(8,128)(2,1)S(1)} copy-done((bf16[2,256,256]{2,1,0:T(8,128)(2,1)S(1)}, bf16[2,256,256]{2,1,0:T(8,128)(2,1)}, u32[]{:S(2)}) %copy-start.8) | copy-done | bytes 262168
  8.4 19.3 %whiten_cross_stack.1 = f32[32,1024]{1,0:T(8,128)S(1)} custom-call(f32[64,2,1024]{2,1,0:T(2,128)S(1)} %copy-done, s32[4,48]{1,0:T(4,128)S(1)} %copy-done.1, s32[2,8]{1,0:T(2,128)S(1)} %copy-done.2, s32[2,16]{1,0:T(2,128)S(1)} %copy-done.3, s32[1]{0:T(128)S(6)} %copy.13.live_ref, bf16[4,256,256]{2,1,0:T(8,128)(2,1)S(1)} %copy-done.7, ...), custom_call_target="tpu_custom_call" | custom-call | flops 2000000000 | bytes 4000000 | tf_op jit(solution)/shard_map/whiten_cross_stack/pallas_call | solution.py:362
  27.7 0.7 %copy.14 = f32[32,1024]{1,0:T(8,128)} copy(f32[32,1024]{1,0:T(8,128)S(1)} %whiten_cross_stack.1) | data formatting | bytes 262144
Async XLA Ops:
  0.0 0.7 %copy-start.9 = (f32[1,512]{1,0:T(1,128)S(1)}, f32[1,512]{1,0:T(1,128)}, u32[]{:S(2)}) copy-start(f32[1,512]{1,0:T(1,128)} %constant.15.clone.share_ref) | copy-start | bytes 6148
  0.0 0.7 %copy-start.2 = (s32[2,8]{1,0:T(2,128)S(1)}, s32[2,8]{1,0:T(2,128)}, u32[]{:S(2)}) copy-start(s32[2,8]{1,0:T(2,128)} %home_ref.1) | copy-start | bytes 196
  0.7 1.0 %copy-start = (f32[64,2,1024]{2,1,0:T(2,128)S(1)}, f32[64,2,1024]{2,1,0:T(2,128)}, u32[]{:S(2)}) copy-start(f32[64,2,1024]{2,1,0:T(2,128)} %traces_hbm.1) | copy-start | bytes 1572868
  1.7 0.7 %copy-start.1 = (s32[4,48]{1,0:T(4,128)S(1)}, s32[4,48]{1,0:T(4,128)}, u32[]{:S(2)}) copy-start(s32[4,48]{1,0:T(4,128)} %needed_ref.1) | copy-start | bytes 2308
  2.4 0.7 %copy-start.3 = (s32[2,16]{1,0:T(2,128)S(1)}, s32[2,16]{1,0:T(2,128)}, u32[]{:S(2)}) copy-start(s32[2,16]{1,0:T(2,128)} %partner_ref.1) | copy-start | bytes 388
  3.1 1.2 %copy-start.4 = (bf16[2,512,512]{2,1,0:T(8,128)(2,1)S(1)}, bf16[2,512,512]{2,1,0:T(8,128)(2,1)}, u32[]{:S(2)}) copy-start(bf16[2,512,512]{2,1,0:T(8,128)(2,1)} %constant.13.clone.fwd_odd_hbm) | copy-start | bytes 3145732
  4.3 1.0 %copy-start.5 = (bf16[2,256,512]{2,1,0:T(8,128)(2,1)S(1)}, bf16[2,256,512]{2,1,0:T(8,128)(2,1)}, u32[]{:S(2)}) copy-start(bf16[2,256,512]{2,1,0:T(8,128)(2,1)} %constant.17.clone.inv_odd_hbm) | copy-start | bytes 1572868
  5.4 1.0 %copy-start.6 = (bf16[512,512]{1,0:T(8,128)(2,1)S(1)}, bf16[512,512]{1,0:T(8,128)(2,1)}, u32[]{:S(2)}) copy-start(bf16[512,512]{1,0:T(8,128)(2,1)} %constant.14.clone.band_hbm) | copy-start | bytes 1572868
  6.4 1.0 %copy-start.7 = (bf16[4,256,256]{2,1,0:T(8,128)(2,1)S(1)}, bf16[4,256,256]{2,1,0:T(8,128)(2,1)}, u32[]{:S(2)}) copy-start(bf16[4,256,256]{2,1,0:T(8,128)(2,1)} %constant.12.clone.fwd_even_hbm) | copy-start | bytes 1572868
  7.5 0.9 %copy-start.8 = (bf16[2,256,256]{2,1,0:T(8,128)(2,1)S(1)}, bf16[2,256,256]{2,1,0:T(8,128)(2,1)}, u32[]{:S(2)}) copy-start(bf16[2,256,256]{2,1,0:T(8,128)(2,1)} %constant.16.clone.inv_even_hbm) | copy-start | bytes 786436

commit v2 on v1

--- a/solution.py
+++ b/solution.py
@@ -49,7 +49,6 @@
     order = np.concatenate([bins_a, bins_b, bins_o])
     inside = np.abs(order[:, None] - order[None, :]) <= BAND_REACH
     band = inside.astype(np.float32).astype(ml_dtypes.bfloat16)
-    share = (1.0 / inside.sum(axis=0, keepdims=True)).astype(np.float32)
     inv_cos, inv_sin = inverse(half, bins_o)
     inv_even = np.stack(
         [
@@ -63,7 +62,7 @@
             for rows in (slice(0, eighth), slice(eighth, None))
         ]
     )
-    return fwd_even, fwd_odd, band, share, inv_even, inv_odd
+    return fwd_even, fwd_odd, band, inv_even, inv_odd
 
 
 def dot(left, right):
@@ -85,17 +84,20 @@
 def kernel(
     dims,
     traces_hbm,
+    needed_hbm,
+    home_hbm,
+    partner_hbm,
+    live_hbm,
+    fwd_even_hbm,
+    fwd_odd_hbm,
+    band_hbm,
+    inv_even_hbm,
+    inv_odd_hbm,
+    out_ref,
     needed_ref,
     home_ref,
     partner_ref,
     live_ref,
-    fwd_even_hbm,
-    fwd_odd_hbm,
-    band_hbm,
-    share_ref,
-    inv_even_hbm,
-    inv_odd_hbm,
-    out_ref,
     traces,
     fwd_even,
     fwd_odd,
@@ -138,11 +140,15 @@
                 (band_hbm, band),
                 (inv_even_hbm, inv_even),
                 (inv_odd_hbm, inv_odd),
+                (needed_hbm, needed_ref),
+                (home_hbm, home_ref),
+                (partner_hbm, partner_ref),
+                (live_hbm, live_ref),
             )
         )
     ]
-    for load in loads:
-        load.start()
+    for i in (6, 7, 8, 0, 1, 2, 3, 4, 5, 9):
+        loads[i].start()
 
     barrier = pltpu.get_barrier_semaphore()
     group_peers = [lax.rem(group + d, groups) for d in range(1, groups)]
@@ -164,6 +170,8 @@
     first_mine = group * chan_dev
     place = lax.broadcasted_iota(jnp.int32, (listing, lanes), 0)
     out_row = lax.broadcasted_iota(jnp.int32, (cap_rows, lanes), 0)
+    for i in (6, 7, 8):
+        loads[i].wait()
     choose = []
     for d in range(groups):
         owner = lax.rem(group + d, groups)
@@ -217,7 +225,14 @@
     power = jnp.concatenate([s[:, :eighth] ** 2 + s[:, eighth:] ** 2 for s in spectra], axis=1)
     loads[3].wait()
     both = dot(jnp.concatenate(halves(power), axis=0), band[...])
-    smooth = (both[:count] + both[count:]) * share_ref[...]
+    spot = lax.broadcasted_iota(jnp.int32, (1, half), 1)
+    bins = jnp.where(
+        spot < eighth,
+        spot * 4,
+        jnp.where(spot < quarter, (spot - eighth) * 4 + 2, (spot - quarter) * 2 + 1),
+    )
+    members = jnp.minimum(bins + BAND_REACH, half - 1) - jnp.maximum(bins - BAND_REACH, 0) + 1
+    smooth = (both[:count] + both[count:]) * (1.0 / members.astype(jnp.float32))
     factor = 1.0 / jnp.sqrt(smooth + 1e-05)
 
     pl.semaphore_wait(barrier, (groups - 1) + 1 + (chips - 1))
@@ -317,6 +332,7 @@
 
     loads[4].wait()
     loads[5].wait()
+    loads[9].wait()
     parts = []
     for k in range(CHUNKS):
         for copy in chip_copies[k]:
@@ -332,7 +348,7 @@
     norm = 1.0 / math.sqrt(samples * win_dev * win_count)
     row = win * share_rows + lax.broadcasted_iota(jnp.int32, (pad_rows, 1), 0)
     block = sum([(row >= b * homes * partners).astype(jnp.int32) for b in range(1, blocks)])
-    gain = jnp.where(block < live_ref[0], norm, 0.0)
+    gain = jnp.where(block < live_ref[...], norm, 0.0)
     out_ref[:, :half] = ((even - odd) * gain)[:share_rows]
     out_ref[:, half:] = ((even + odd) * gain)[:share_rows]
 
@@ -353,18 +369,21 @@
     share_rows = blocks * homes * partners // win_count
     pad_rows = max(share_rows, 16)
     quarter = samples // 4
-    fwd_even, fwd_odd, band, share, inv_even, inv_odd = tables(samples)
+    fwd_even, fwd_odd, band, inv_even, inv_odd = tables(samples)
     dims = (groups, win_count, chan_dev, win_dev, samples, listing, cap, cap_rows, blocks, homes, partners)
     vmem = pl.BlockSpec(memory_space=pltpu.VMEM)
-    smem = pl.BlockSpec(memory_space=pltpu.SMEM)
-    hbm = pl.BlockSpec(memory_space=pl.ANY)
+    hbm = pl.BlockSpec(memory_space=pltpu.HBM)
     bf16, f32 = jnp.bfloat16, jnp.float32
     return pl.pallas_call(
         functools.partial(kernel, dims),
         out_shape=jax.ShapeDtypeStruct((share_rows, samples), f32),
-        in_specs=[hbm, vmem, vmem, vmem, smem, hbm, hbm, hbm, vmem, hbm, hbm],
+        in_specs=[hbm] * 10,
         out_specs=vmem,
         scratch_shapes=[
+            pltpu.VMEM(needed.shape, jnp.int32),
+            pltpu.VMEM(home_slot.shape, jnp.int32),
+            pltpu.VMEM(partner_slot.shape, jnp.int32),
+            pltpu.VMEM((1, 1), jnp.int32),
             pltpu.VMEM(traces.shape, f32),
             pltpu.VMEM(fwd_even.shape, bf16),
             pltpu.VMEM(fwd_odd.shape, bf16),
@@ -379,7 +398,7 @@
             pltpu.VMEM((CHUNKS, chips, pad_rows, quarter), f32),
             pltpu.VMEM((CHUNKS, chips, pad_rows, quarter), bf16),
             pltpu.VMEM((CHUNKS, chips - 1, pad_rows, quarter), bf16),
-            pltpu.SemaphoreType.DMA((6,)),
+            pltpu.SemaphoreType.DMA((10,)),
             pltpu.SemaphoreType.DMA((CHUNKS, groups - 1)),
             pltpu.SemaphoreType.DMA((CHUNKS, groups - 1)),
             pltpu.SemaphoreType.DMA((CHUNKS,)),
@@ -388,7 +407,7 @@
             pltpu.SemaphoreType.DMA((CHUNKS, chips - 1)),
         ],
         compiler_params=pltpu.CompilerParams(
-            collective_id=0, has_side_effects=True, vmem_limit_bytes=40 * 1024 * 1024
+            collective_id=0, has_side_effects=True, vmem_limit_bytes=64 * 1024 * 1024
         ),
         cost_estimate=pl.CostEstimate(
             flops=2_000_000_000, bytes_accessed=4_000_000, transcendentals=100_000
@@ -399,11 +418,10 @@
         needed,
         home_slot,
         partner_slot,
-        live_blocks,
+        live_blocks.reshape(1, 1),
         jnp.asarray(fwd_even),
         jnp.asarray(fwd_odd),
         jnp.asarray(band),
-        jnp.asarray(share),
         jnp.asarray(inv_even),
         jnp.asarray(inv_odd),
     )

time: 28.8 us -> 23 us (0.80)
  local copies, waits for them, and re-layouts: 8.36 us -> 1.57 us
  Pallas kernels: 19.3 us -> 20.6 us
    unnamed x21 -> x1, local copies, waits for them, and re-layouts: 8.36 us -> 1.57 us
    pallas_call x1, Pallas kernels: 19.3 us -> 20.6 us  [body(): pl.pallas_call(functools.partial(kernel, dims), out_shape=jax.ShapeDtypeS...]
where the time goes in v2:
time: 23 us; the launch traced here: 22.8 us
  Pallas kernels  20.6 us (90%)
  local copies, waits for them, and re-layouts  1.57 us (7%)
  between operations  0.66 us (3%)
    pallas_call x1, Pallas kernels, body(): pl.pallas_call(functools.partial(kernel, dims), out_shape=jax.ShapeDtypeS...  20.6 us
    unnamed x1, local copies, waits for them, and re-layouts  1.57 us

profile of v2, /device:TPU:0, one launch (start us, length us, event | category | flops | bytes accessed | tf_op | source)
XLA Modules:
  0.0 22.8 jit_solution(9376217175035426735)
XLA Ops:
  0.7 20.6 %whiten_cross_stack.1 = f32[32,1024]{1,0:T(8,128)} custom-call(f32[64,2,1024]{2,1,0:T(2,128)} %traces_hbm.1, s32[4,48]{1,0:T(4,128)} %needed_hbm.1, s32[2,8]{1,0:T(2,128)} %home_hbm.1, s32[2,16]{1,0:T(2,128)} %partner_hbm.1, s32[1,1]{1,0:T(1,128)} %bitcast.1.live_hbm, bf16[4,256,256]{2,1,0:T(8,128)(2,1)} %constant.10.clone.fwd_even_hbm, ...), custom_call_target="tpu_custom_call" | custom-call | flops 2000000000 | bytes 4000000 | tf_op jit(solution)/shard_map/whiten_cross_stack/pallas_call | solution.py:377
  21.3 1.6 %copy.13 = f32[32,1024]{1,0:T(8,128)} copy(f32[32,1024]{1,0:T(8,128)} %whiten_cross_stack.1) | data formatting | bytes 262144

commit v3 on v2

v3 whole, which is shorter than its diff:
```python
import functools
import math

import jax
import jax.numpy as jnp
import ml_dtypes
import numpy as np
from jax import lax
from jax.experimental import pallas as pl
from jax.experimental.pallas import tpu as pltpu
from jax.sharding import PartitionSpec as P

MESH = pl.DeviceIdType.MESH
BAND_REACH = 64


def split_table(table):
    high = table.astype(np.float32).astype(ml_dtypes.bfloat16)
    low = (table - high.astype(np.float64)).astype(np.float32).astype(ml_dtypes.bfloat16)
    return high, low


@functools.lru_cache(maxsize=None)
def tables(samples):
    quarter, half = samples // 4, samples // 2
    eighth = samples // 8
    bins_a = np.arange(0, half, 4)
    bins_b = np.arange(2, half, 4)
    bins_o = np.arange(1, half, 2)

    def forward(length, bins):
        phase = (np.arange(length)[:, None] * bins[None, :] % samples) * (2.0 * np.pi / samples)
        return np.cos(phase), -np.sin(phase)

    def inverse(length, bins):
        phase = (bins[:, None] * np.arange(length)[None, :] % samples) * (2.0 * np.pi / samples)
        weight = np.where(bins == 0, 1.0, 2.0)[:, None]
        return weight * np.cos(phase), -weight * np.sin(phase)

    odd_cos, odd_sin = forward(half, bins_o)
    fwd_a = np.concatenate(forward(quarter, bins_a), axis=1)
    fwd_b = np.concatenate(forward(quarter, bins_b), axis=1)
    fwd_o = np.concatenate(
        [odd_cos[:, :eighth], odd_sin[:, :eighth], odd_cos[:, eighth:], odd_sin[:, eighth:]], axis=1
    )
    fwd_even = np.stack([x for t in (fwd_a, fwd_b) for x in split_table(t)])
    fwd_odd = np.stack(split_table(fwd_o))
    order = np.concatenate([bins_a, bins_b, bins_o])
    inside = np.abs(order[:, None] - order[None, :]) <= BAND_REACH
    band = inside.astype(np.float32).astype(ml_dtypes.bfloat16)
    inv_cos, inv_sin = inverse(half, bins_o)
    inv_even = np.stack(
        [
            split_table(np.concatenate(inverse(quarter, bins), axis=0))[0]
            for bins in (bins_a, bins_b)
        ]
    )
    inv_odd = np.stack(
        [
            split_table(np.concatenate([inv_cos[rows], inv_sin[rows]], axis=0))[0]
            for rows in (slice(0, eighth), slice(eighth, None))
        ]
    )
    return fwd_even, fwd_odd, band, inv_even, inv_odd


def dot(left, right):
    return jnp.dot(left, right, preferred_element_type=jnp.float32)


def halves(value):
    high = value.astype(jnp.bfloat16)
    low = (value - high.astype(jnp.float32)).astype(jnp.bfloat16)
    return high, low


def as_column(row):
    n = row.shape[1]
    eye = lax.broadcasted_iota(jnp.int32, (n, n), 0) == lax.broadcasted_iota(jnp.int32, (n, n), 1)
    return jnp.sum(jnp.where(eye, jnp.broadcast_to(row, (n, n)), 0), axis=1, keepdims=True)


def kernel(
    dims,
    traces_hbm,
    needed_hbm,
    home_hbm,
    partner_hbm,
    fwd_even_hbm,
    fwd_odd_hbm,
    band_hbm,
    inv_even_hbm,
    inv_odd_hbm,
    out_ref,
    needed_ref,
    home_ref,
    partner_ref,
    traces,
    fwd_even,
    fwd_odd,
    band,
    inv_even,
    inv_odd,
    listed_out,
    listed_in,
    terms,
    terms_out,
    terms_in,
    load_sem,
    list_send,
    list_recv,
    term_send,
    term_recv,
):
    groups, win_count, chan_dev, win_dev, samples, listing, cap, cap_rows, blocks, homes, partners = dims
    chips = win_count // 2
    pairs = blocks * homes * partners
    share_rows = pairs // win_count
    pad_rows = terms.shape[2]
    quarter, half, eighth = samples // 4, samples // 2, samples // 8
    group = lax.axis_index("chan")
    win = lax.axis_index("win")
    chip, core = win // 2, win % 2

    loads = [
        pltpu.make_async_copy(src, dst, load_sem.at[i])
        for i, (src, dst) in enumerate(
            (
                (traces_hbm, traces),
                (fwd_even_hbm, fwd_even),
                (fwd_odd_hbm, fwd_odd),
                (band_hbm, band),
                (inv_even_hbm, inv_even),
                (inv_odd_hbm, inv_odd),
                (needed_hbm, needed_ref),
                (home_hbm, home_ref),
                (partner_hbm, partner_ref),
            )
        )
    ]
    for i in (6, 7, 8, 0, 1, 2, 3, 4, 5):
        loads[i].start()

    barrier = pltpu.get_barrier_semaphore()
    cores = (core, 1 - core)
    list_peers = [(d, s) for s in range(2) for d in range(groups) if d or s]
    term_peers = [(d, s) for d in reversed(range(chips)) for s in range(2) if d or s]

    def list_id(d, s):
        return {"chan": lax.rem(group + d, groups), "win": chip * 2 + cores[s]}

    def term_index(d, s):
        return lax.rem(chip + d, chips) * 2 + cores[s]

    greeted = [list_id(d, s) for d, s in list_peers]
    greeted += [{"win": term_index(d, s)} for d, s in term_peers if d]
    for peer in greeted:
        pl.semaphore_signal(barrier, inc=1, device_id=peer, device_id_type=MESH)

    lanes = win_dev * chan_dev
    lane = lax.broadcasted_iota(jnp.int32, (1, lanes), 1)
    lane_win = sum([(lane >= w * chan_dev).astype(jnp.int32) for w in range(1, win_dev)])
    lane_chan = lane - lane_win * chan_dev
    first_mine = group * chan_dev
    place = lax.broadcasted_iota(jnp.int32, (listing, lanes), 0)
    out_row = lax.broadcasted_iota(jnp.int32, (cap_rows, lanes), 0)
    for i in (6, 7, 8):
        loads[i].wait()
    choose = []
    for d in range(groups):
        owner = lax.rem(group + d, groups)
        column = as_column(needed_ref[pl.ds(owner, 1), :])
        hit = column == (lane_chan + first_mine)
        found = jnp.sum(jnp.where(hit, place + 1, 0), axis=0, keepdims=True)
        begin = jnp.sum((column < first_mine).astype(jnp.int32), axis=0, keepdims=True)
        target = jnp.where(found > 0, found - 1 - begin + lane_win * cap, -1)
        choose.append(jnp.where(out_row == target, 1.0, 0.0))
    choose = jnp.concatenate(choose, axis=0).astype(jnp.bfloat16)

    loads[0].wait()
    rows = jnp.concatenate([traces[:, w, :] for w in range(win_dev)], axis=0)
    count = rows.shape[0]
    folded = rows[:, :half] + rows[:, half:]
    odd_in = rows[:, :half] - rows[:, half:]
    even_in = (folded[:, :quarter] + folded[:, quarter:], folded[:, :quarter] - folded[:, quarter:])

    def transform(value, high_table, low_table):
        high, low = halves(value)
        both = dot(jnp.concatenate([high, low], axis=0), high_table)
        return both[:count] + both[count:] + dot(high, low_table)

    loads[1].wait()
    spectra = [
        transform(even_in[0], fwd_even[0], fwd_even[1]),
        transform(even_in[1], fwd_even[2], fwd_even[3]),
    ]
    loads[2].wait()
    odd_out = transform(odd_in, fwd_odd[0], fwd_odd[1])
    spectra += [odd_out[:, :quarter], odd_out[:, quarter:]]
    power = jnp.concatenate([s[:, :eighth] ** 2 + s[:, eighth:] ** 2 for s in spectra], axis=1)
    loads[3].wait()
    both = dot(jnp.concatenate(halves(power), axis=0), band[...])
    spot = lax.broadcasted_iota(jnp.int32, (1, half), 1)
    bins = jnp.where(
        spot < eighth,
        spot * 4,
        jnp.where(spot < quarter, (spot - eighth) * 4 + 2, (spot - quarter) * 2 + 1),
    )
    members = jnp.minimum(bins + BAND_REACH, half - 1) - jnp.maximum(bins - BAND_REACH, 0) + 1
    smooth = (both[:count] + both[count:]) * (1.0 / members.astype(jnp.float32))
    factor = 1.0 / jnp.sqrt(smooth + 1e-05)

    pl.semaphore_wait(barrier, len(greeted))

    list_copies = []
    for h in range(2):
        for k in (h, 2 + h):
            scale = factor[:, k * eighth : (k + 1) * eighth]
            whitened = jnp.concatenate(
                [spectra[k][:, :eighth] * scale, spectra[k][:, eighth:] * scale], axis=1
            ).astype(jnp.bfloat16)
            chosen = dot(choose, whitened).astype(jnp.bfloat16)
            for d in range(groups):
                listed_out[k, d] = chosen[d * cap_rows : (d + 1) * cap_rows]
        copies = []
        for n, (d, s) in enumerate(list_peers):
            copies.append(
                pltpu.make_async_remote_copy(
                    src_ref=listed_out.at[cores[s] * 2 + h, d],
                    dst_ref=listed_in.at[h, s, d],
                    send_sem=list_send.at[h, n],
                    recv_sem=list_recv.at[h, n],
                    device_id=list_id(d, s),
                    device_id_type=MESH,
                )
            )
            copies[-1].start()
        list_copies.append(copies)
        listed_in[h, 0, 0] = listed_out[core * 2 + h, 0]

    mine = needed_ref[pl.ds(group, 1), :]
    arrived = lax.broadcasted_iota(jnp.int32, (1, groups * cap_rows), 1)
    code = jnp.full((1, groups * cap_rows), -1, jnp.int32)
    for d in range(groups):
        source = lax.rem(group + groups - d, groups)
        begin = jnp.sum(
            (mine < source * chan_dev).astype(jnp.int32), axis=1, keepdims=True
        )
        for w in range(win_dev):
            low = d * cap_rows + w * cap
            within = (arrived >= low) & (arrived < low + cap)
            code = jnp.where(within, arrived - low + begin + w * listing, code)
    wanted = [as_column(partner_ref[b : b + 1, :]) for b in range(blocks)]
    wanted += [as_column(home_ref[b : b + 1, :]) for b in range(blocks)]
    wanted = jnp.concatenate(wanted, axis=0)
    per_win = blocks * (homes + partners)
    wanted = jnp.concatenate([wanted + w * listing for w in range(win_dev)], axis=0)
    pick = jnp.where(wanted == code, 1.0, 0.0).astype(jnp.bfloat16)

    term_copies = []
    piece = min(partners, share_rows)
    for h in range(2):
        for copy in list_copies[h]:
            copy.wait_recv()
        tables = [dot(pick, listed_in[h, s].reshape(groups * cap_rows, quarter)) for s in range(2)]
        for b in range(blocks):
            for i in range(homes):
                real = imag = None
                for table in tables:
                    for w in range(win_dev):
                        at = w * per_win + blocks * partners + b * homes + i
                        home_re = table[at : at + 1, :eighth]
                        home_im = table[at : at + 1, eighth:]
                        at = w * per_win + b * partners
                        part_re = table[at : at + partners, :eighth]
                        part_im = table[at : at + partners, eighth:]
                        add_re = home_re * part_re + home_im * part_im
                        add_im = home_im * part_re - home_re * part_im
                        real = add_re if real is None else real + add_re
                        imag = add_im if imag is None else imag + add_im
                term = jnp.concatenate([real, imag], axis=1)
                for j in range(0, partners, piece):
                    row = (b * homes + i) * partners + j
                    owner, inner = row // share_rows, row % share_rows
                    terms[h, owner, inner : inner + piece, :] = term[j : j + piece]
        terms_out[h] = terms[h].astype(jnp.bfloat16)
        copies = []
        for n, (d, s) in enumerate(term_peers):
            copies.append(
                pltpu.make_async_remote_copy(
                    src_ref=terms_out.at[h, term_index(d, s)],
                    dst_ref=terms_in.at[h, n],
                    send_sem=term_send.at[h, n],
                    recv_sem=term_recv.at[h, n],
                    device_id={"win": term_index(d, s)},
                    device_id_type=MESH,
                )
            )
            copies[-1].start()
        term_copies.append(copies)

    loads[4].wait()
    loads[5].wait()
    parts = [None] * 4
    for h in range(2):
        total = [terms[h, win], None]
        for n, (d, s) in enumerate(term_peers):
            term_copies[h][n].wait_recv()
            arrival = terms_in[h, n].astype(jnp.float32)
            total[s] = arrival if total[s] is None else total[s] + arrival
        for k, value in (
            (h, jnp.where(core == 0, total[0], total[1])),
            (2 + h, jnp.where(core == 0, total[1], total[0])),
        ):
            table = inv_even[h] if k < 2 else inv_odd[h]
            both = dot(jnp.concatenate(halves(value), axis=0), table)
            parts[k] = both[:pad_rows] + both[pad_rows:]
    even = jnp.concatenate([parts[0] + parts[1], parts[0] - parts[1]], axis=1)
    odd = parts[2] + parts[3]
    norm = 1.0 / math.sqrt(samples * win_dev * win_count)
    out_ref[:, :half] = ((even - odd) * norm)[:share_rows]
    out_ref[:, half:] = ((even + odd) * norm)[:share_rows]

    for copies in list_copies + term_copies:
        for copy in copies:
            copy.wait_send()


def body(traces, needed, home_slot, partner_slot, live_blocks):
    chan_dev, win_dev, samples = traces.shape
    groups, win_count = lax.axis_size("chan"), lax.axis_size("win")
    listing = needed.shape[1]
    cap = 2 * listing // groups
    cap_rows = -(-win_dev * cap // 16) * 16
    blocks, homes = home_slot.shape
    partners = partner_slot.shape[1]
    share_rows = blocks * homes * partners // win_count
    pad_rows = max(share_rows, 16)
    quarter = samples // 4
    fwd_even, fwd_odd, band, inv_even, inv_odd = tables(samples)
    dims = (groups, win_count, chan_dev, win_dev, samples, listing, cap, cap_rows, blocks, homes, partners)
    vmem = pl.BlockSpec(memory_space=pltpu.VMEM)
    hbm = pl.BlockSpec(memory_space=pltpu.HBM)
    bf16, f32 = jnp.bfloat16, jnp.float32
    stacked = pl.pallas_call(
        functools.partial(kernel, dims),
        out_shape=jax.ShapeDtypeStruct((share_rows, samples), f32),
        in_specs=[hbm] * 9,
        out_specs=vmem,
        scratch_shapes=[
            pltpu.VMEM(needed.shape, jnp.int32),
            pltpu.VMEM(home_slot.shape, jnp.int32),
            pltpu.VMEM(partner_slot.shape, jnp.int32),
            pltpu.VMEM(traces.shape, f32),
            pltpu.VMEM(fwd_even.shape, bf16),
            pltpu.VMEM(fwd_odd.shape, bf16),
            pltpu.VMEM(band.shape, bf16),
            pltpu.VMEM(inv_even.shape, bf16),
            pltpu.VMEM(inv_odd.shape, bf16),
            pltpu.VMEM((4, groups, cap_rows, quarter), bf16),
            pltpu.VMEM((2, 2, groups, cap_rows, quarter), bf16),
            pltpu.VMEM((2, win_count, pad_rows, quarter), f32),
            pltpu.VMEM((2, win_count, pad_rows, quarter), bf16),
            pltpu.VMEM((2, win_count - 1, pad_rows, quarter), bf16),
            pltpu.SemaphoreType.DMA((9,)),
            pltpu.SemaphoreType.DMA((2, 2 * groups - 1)),
            pltpu.SemaphoreType.DMA((2, 2 * groups - 1)),
            pltpu.SemaphoreType.DMA((2, win_count - 1)),
            pltpu.SemaphoreType.DMA((2, win_count - 1)),
        ],
        compiler_params=pltpu.CompilerParams(
            collective_id=0, has_side_effects=True, vmem_limit_bytes=64 * 1024 * 1024
        ),
        cost_estimate=pl.CostEstimate(
            flops=2_000_000_000, bytes_accessed=4_000_000, transcendentals=100_000
        ),
        name="whiten_cross_stack",
    )(
        traces,
        needed,
        home_slot,
        partner_slot,
        jnp.asarray(fwd_even),
        jnp.asarray(fwd_odd),
        jnp.asarray(band),
        jnp.asarray(inv_even),
        jnp.asarray(inv_odd),
    )
    row = lax.axis_index("win") * share_rows + lax.broadcasted_iota(jnp.int32, (share_rows, 1), 0)
    return stacked * (row // (homes * partners) < live_blocks[0]).astype(f32)


def solution(mesh):
    placed = (P("chan", "win", None), P(), P("chan", None), P("chan", None), P("chan"))
    return jax.shard_map(
        body, mesh=mesh, in_specs=placed, out_specs=P(("chan", "win"), None), check_vma=False
    )
```

time: 23 us -> 23 us (level)
  other arithmetic: 0 us -> 2.16 us
  local copies, waits for them, and re-layouts: 1.57 us -> 0 us
  Pallas kernels: 20.6 us -> 20 us
    mul x0 -> x1, other arithmetic: none -> 1.64 us  [body(): return stacked * (row // (homes * partners) < live_blocks[0]).astype(f32)]
    unnamed x1 -> x0, local copies, waits for them, and re-layouts: 1.57 us -> none
    pallas_call x1, Pallas kernels: 20.6 us -> 20 us  [body(): pl.pallas_call(functools.partial(kernel, dims), out_shape=jax.ShapeDtypeS...]
    convert_element_type x0 -> x1, other arithmetic: none -> 0.52 us  [body(): return stacked * (row // (homes * partners) < live_blocks[0]).astype(f32)]
where the time goes in v3:
time: 23 us; the launch traced here: 22.8 us
  Pallas kernels  20 us (87%)
  other arithmetic  2.16 us (9%)
  between operations  0.66 us (3%)
    pallas_call x1, Pallas kernels, body(): pl.pallas_call(functools.partial(kernel, dims), out_shape=jax.ShapeDtypeS...  20 us
    mul x1, other arithmetic, body(): return stacked * (row // (homes * partners) < live_blocks[0]).astype(f32)  1.64 us
    convert_element_type x1, other arithmetic, body(): return stacked * (row // (homes * partners) < live_blocks[0]).astype(f32)  0.52 us

profile of v3, /device:TPU:0, one launch (start us, length us, event | category | flops | bytes accessed | tf_op | source)
XLA Modules:
  0.0 22.8 jit_solution(9525593101481053702)
XLA Ops:
  0.7 0.5 %compare_convert_fusion = f32[32]{0:T(128)} fusion(s32[]{:T(128)} %bitcast.1, s32[]{:T(128)S(6)} %mul.11), kind=kLoop, calls=%fused_computation.1 | loop fusion | flops 576 | bytes 136 | tf_op jit(solution)/shard_map/convert_element_type | solution.py:390
  1.2 20.0 %whiten_cross_stack.1 = f32[32,1024]{1,0:T(8,128)} custom-call(f32[64,2,1024]{2,1,0:T(2,128)} %traces_hbm.1, s32[4,48]{1,0:T(4,128)} %needed_hbm.1, s32[2,8]{1,0:T(2,128)} %home_hbm.1, s32[2,16]{1,0:T(2,128)} %partner_hbm.1, bf16[4,256,256]{2,1,0:T(8,128)(2,1)} %constant.32.clone.fwd_even_hbm, bf16[2,512,512]{2,1,0:T(8,128)(2,1)} %constant.33.clone.fwd_odd_hbm, ...), custom_call_target="tpu_custom_call" | custom-call | flops 2000000000 | bytes 4000000 | tf_op jit(solution)/shard_map/whiten_cross_stack/pallas_call | solution.py:345
  21.2 1.6 %broadcast_multiply_fusion = f32[32,1024]{1,0:T(8,128)} fusion(f32[32,1024]{1,0:T(8,128)} %whiten_cross_stack.1, f32[32]{0:T(128)} %compare_convert_fusion), kind=kLoop, calls=%fused_computation | loop fusion | flops 32768 | bytes 262272 | tf_op jit(solution)/shard_map/mul | solution.py:390

commit v4 on v3

--- a/solution.py
+++ b/solution.py
@@ -12,6 +12,7 @@
 
 MESH = pl.DeviceIdType.MESH
 BAND_REACH = 64
+PIECES = 4
 
 
 def split_table(table):
@@ -48,19 +49,17 @@
     order = np.concatenate([bins_a, bins_b, bins_o])
     inside = np.abs(order[:, None] - order[None, :]) <= BAND_REACH
     band = inside.astype(np.float32).astype(ml_dtypes.bfloat16)
-    inv_cos, inv_sin = inverse(half, bins_o)
-    inv_even = np.stack(
-        [
-            split_table(np.concatenate(inverse(quarter, bins), axis=0))[0]
-            for bins in (bins_a, bins_b)
+    piece = eighth // 2
+
+    def pieces(length, bins):
+        cos, sin = inverse(length, bins)
+        return [
+            split_table(np.concatenate([cos[at : at + piece], sin[at : at + piece]], axis=0))[0]
+            for at in range(0, len(bins), piece)
         ]
-    )
-    inv_odd = np.stack(
-        [
-            split_table(np.concatenate([inv_cos[rows], inv_sin[rows]], axis=0))[0]
-            for rows in (slice(0, eighth), slice(eighth, None))
-        ]
-    )
+
+    inv_even = np.stack(pieces(quarter, bins_a) + pieces(quarter, bins_b))
+    inv_odd = np.stack(pieces(half, bins_o))
     return fwd_even, fwd_odd, band, inv_even, inv_odd
 
 
@@ -86,6 +85,7 @@
     needed_hbm,
     home_hbm,
     partner_hbm,
+    live_ref,
     fwd_even_hbm,
     fwd_odd_hbm,
     band_hbm,
@@ -208,25 +208,37 @@
     )
     members = jnp.minimum(bins + BAND_REACH, half - 1) - jnp.maximum(bins - BAND_REACH, 0) + 1
     smooth = (both[:count] + both[count:]) * (1.0 / members.astype(jnp.float32))
-    factor = 1.0 / jnp.sqrt(smooth + 1e-05)
+    factor = lax.rsqrt(smooth + 1e-05)
 
     pl.semaphore_wait(barrier, len(greeted))
 
+    first_half = lax.broadcasted_iota(jnp.int32, (1, eighth), 1) < eighth // 2
+
+    def swap(value):
+        return pltpu.roll(value, eighth // 2, 1)
+
     list_copies = []
-    for h in range(2):
-        for k in (h, 2 + h):
-            scale = factor[:, k * eighth : (k + 1) * eighth]
-            whitened = jnp.concatenate(
-                [spectra[k][:, :eighth] * scale, spectra[k][:, eighth:] * scale], axis=1
-            ).astype(jnp.bfloat16)
-            chosen = dot(choose, whitened).astype(jnp.bfloat16)
-            for d in range(groups):
-                listed_out[k, d] = chosen[d * cap_rows : (d + 1) * cap_rows]
+    for h in range(PIECES):
+        if h % 2 == 0:
+            for half_at in range(2):
+                k = half_at * 2 + h // 2
+                scale = factor[:, k * eighth : (k + 1) * eighth]
+                whitened = jnp.concatenate(
+                    [spectra[k][:, :eighth] * scale, spectra[k][:, eighth:] * scale], axis=1
+                ).astype(jnp.bfloat16)
+                chosen = dot(choose, whitened)
+                real, imag = chosen[:, :eighth], chosen[:, eighth:]
+                for j, value in enumerate(
+                    (jnp.where(first_half, real, swap(imag)), jnp.where(first_half, swap(real), imag))
+                ):
+                    value = value.astype(jnp.bfloat16)
+                    for d in range(groups):
+                        listed_out[half_at, h + j, d] = value[d * cap_rows : (d + 1) * cap_rows]
         copies = []
         for n, (d, s) in enumerate(list_peers):
             copies.append(
                 pltpu.make_async_remote_copy(
-                    src_ref=listed_out.at[cores[s] * 2 + h, d],
+                    src_ref=listed_out.at[cores[s], h, d],
                     dst_ref=listed_in.at[h, s, d],
                     send_sem=list_send.at[h, n],
                     recv_sem=list_recv.at[h, n],
@@ -236,7 +248,7 @@
             )
             copies[-1].start()
         list_copies.append(copies)
-        listed_in[h, 0, 0] = listed_out[core * 2 + h, 0]
+        listed_in[h, 0, 0] = listed_out[core, h, 0]
 
     mine = needed_ref[pl.ds(group, 1), :]
     arrived = lax.broadcasted_iota(jnp.int32, (1, groups * cap_rows), 1)
@@ -259,26 +271,24 @@
 
     term_copies = []
     piece = min(partners, share_rows)
-    for h in range(2):
+    for h in range(PIECES):
         for copy in list_copies[h]:
             copy.wait_recv()
-        tables = [dot(pick, listed_in[h, s].reshape(groups * cap_rows, quarter)) for s in range(2)]
+        tables = [dot(pick, listed_in[h, s].reshape(groups * cap_rows, eighth)) for s in range(2)]
+        swapped = [swap(table) for table in tables]
         for b in range(blocks):
             for i in range(homes):
-                real = imag = None
-                for table in tables:
+                straight = crossed = None
+                for table, other in zip(tables, swapped):
                     for w in range(win_dev):
                         at = w * per_win + blocks * partners + b * homes + i
-                        home_re = table[at : at + 1, :eighth]
-                        home_im = table[at : at + 1, eighth:]
+                        home = table[at : at + 1]
                         at = w * per_win + b * partners
-                        part_re = table[at : at + partners, :eighth]
-                        part_im = table[at : at + partners, eighth:]
-                        add_re = home_re * part_re + home_im * part_im
-                        add_im = home_im * part_re - home_re * part_im
-                        real = add_re if real is None else real + add_re
-                        imag = add_im if imag is None else imag + add_im
-                term = jnp.concatenate([real, imag], axis=1)
+                        add = home * table[at : at + partners]
+                        straight = add if straight is None else straight + add
+                        add = home * other[at : at + partners]
+                        crossed = add if crossed is None else crossed + add
+                term = jnp.where(first_half, straight + swap(straight), crossed - swap(crossed))
                 for j in range(0, partners, piece):
                     row = (b * homes + i) * partners + j
                     owner, inner = row // share_rows, row % share_rows
@@ -301,23 +311,25 @@
 
     loads[4].wait()
     loads[5].wait()
-    parts = [None] * 4
-    for h in range(2):
+    parts = [[], [], []]
+    for h in range(PIECES):
         total = [terms[h, win], None]
         for n, (d, s) in enumerate(term_peers):
             term_copies[h][n].wait_recv()
             arrival = terms_in[h, n].astype(jnp.float32)
             total[s] = arrival if total[s] is None else total[s] + arrival
-        for k, value in (
-            (h, jnp.where(core == 0, total[0], total[1])),
-            (2 + h, jnp.where(core == 0, total[1], total[0])),
+        for value, table, part in (
+            (jnp.where(core == 0, total[0], total[1]), inv_even[h], h // 2),
+            (jnp.where(core == 0, total[1], total[0]), inv_odd[h], 2),
         ):
-            table = inv_even[h] if k < 2 else inv_odd[h]
             both = dot(jnp.concatenate(halves(value), axis=0), table)
-            parts[k] = both[:pad_rows] + both[pad_rows:]
+            parts[part].append(both[:pad_rows] + both[pad_rows:])
+    parts = [sum(part) for part in parts]
     even = jnp.concatenate([parts[0] + parts[1], parts[0] - parts[1]], axis=1)
-    odd = parts[2] + parts[3]
+    odd = parts[2]
     norm = 1.0 / math.sqrt(samples * win_dev * win_count)
+    row = win * share_rows + lax.broadcasted_iota(jnp.int32, (pad_rows, 1), 0)
+    norm = jnp.where(row < live_ref[0] * (homes * partners), norm, 0.0)
     out_ref[:, :half] = ((even - odd) * norm)[:share_rows]
     out_ref[:, half:] = ((even + odd) * norm)[:share_rows]
 
@@ -336,16 +348,17 @@
     partners = partner_slot.shape[1]
     share_rows = blocks * homes * partners // win_count
     pad_rows = max(share_rows, 16)
-    quarter = samples // 4
+    eighth = samples // 8
     fwd_even, fwd_odd, band, inv_even, inv_odd = tables(samples)
     dims = (groups, win_count, chan_dev, win_dev, samples, listing, cap, cap_rows, blocks, homes, partners)
     vmem = pl.BlockSpec(memory_space=pltpu.VMEM)
+    smem = pl.BlockSpec(memory_space=pltpu.SMEM)
     hbm = pl.BlockSpec(memory_space=pltpu.HBM)
     bf16, f32 = jnp.bfloat16, jnp.float32
-    stacked = pl.pallas_call(
+    return pl.pallas_call(
         functools.partial(kernel, dims),
         out_shape=jax.ShapeDtypeStruct((share_rows, samples), f32),
-        in_specs=[hbm] * 9,
+        in_specs=[hbm] * 4 + [smem] + [hbm] * 5,
         out_specs=vmem,
         scratch_shapes=[
             pltpu.VMEM(needed.shape, jnp.int32),
@@ -357,16 +370,16 @@
             pltpu.VMEM(band.shape, bf16),
             pltpu.VMEM(inv_even.shape, bf16),
             pltpu.VMEM(inv_odd.shape, bf16),
-            pltpu.VMEM((4, groups, cap_rows, quarter), bf16),
-            pltpu.VMEM((2, 2, groups, cap_rows, quarter), bf16),
-            pltpu.VMEM((2, win_count, pad_rows, quarter), f32),
-            pltpu.VMEM((2, win_count, pad_rows, quarter), bf16),
-            pltpu.VMEM((2, win_count - 1, pad_rows, quarter), bf16),
+            pltpu.VMEM((2, PIECES, groups, cap_rows, eighth), bf16),
+            pltpu.VMEM((PIECES, 2, groups, cap_rows, eighth), bf16),
+            pltpu.VMEM((PIECES, win_count, pad_rows, eighth), f32),
+            pltpu.VMEM((PIECES, win_count, pad_rows, eighth), bf16),
+            pltpu.VMEM((PIECES, win_count - 1, pad_rows, eighth), bf16),
             pltpu.SemaphoreType.DMA((9,)),
-            pltpu.SemaphoreType.DMA((2, 2 * groups - 1)),
-            pltpu.SemaphoreType.DMA((2, 2 * groups - 1)),
-            pltpu.SemaphoreType.DMA((2, win_count - 1)),
-            pltpu.SemaphoreType.DMA((2, win_count - 1)),
+            pltpu.SemaphoreType.DMA((PIECES, 2 * groups - 1)),
+            pltpu.SemaphoreType.DMA((PIECES, 2 * groups - 1)),
+            pltpu.SemaphoreType.DMA((PIECES, win_count - 1)),
+            pltpu.SemaphoreType.DMA((PIECES, win_count - 1)),
         ],
         compiler_params=pltpu.CompilerParams(
             collective_id=0, has_side_effects=True, vmem_limit_bytes=64 * 1024 * 1024
@@ -380,16 +393,13 @@
         needed,
         home_slot,
         partner_slot,
+        live_blocks,
         jnp.asarray(fwd_even),
         jnp.asarray(fwd_odd),
         jnp.asarray(band),
         jnp.asarray(inv_even),
         jnp.asarray(inv_odd),
     )
-    row = lax.axis_index("win") * share_rows + lax.broadcasted_iota(jnp.int32, (share_rows, 1), 0)
-    return stacked * (row // (homes * partners) < live_blocks[0]).astype(f32)
-
-
 def solution(mesh):
     placed = (P("chan", "win", None), P(), P("chan", None), P("chan", None), P("chan"))
     return jax.shard_map(

time: 23 us -> 22.7 us (0.987)
  other arithmetic: 2.16 us -> 0 us
  local copies, waits for them, and re-layouts: 0 us -> 1.57 us
  Pallas kernels: 20 us -> 20.3 us
    mul x1 -> x0, other arithmetic: 1.64 us -> none  [body(): return stacked * (row // (homes * partners) < live_blocks[0]).astype(f32)]
    unnamed x0 -> x1, local copies, waits for them, and re-layouts: none -> 1.57 us
    convert_element_type x1 -> x0, other arithmetic: 0.52 us -> none  [body(): return stacked * (row // (homes * partners) < live_blocks[0]).astype(f32)]
    pallas_call x1, Pallas kernels: 20 us -> 20.3 us  [body(): pl.pallas_call(functools.partial(kernel, dims), out_shape=jax.ShapeDtypeS...]
where the time goes in v4:
time: 22.7 us; the launch traced here: 22.5 us
  Pallas kernels  20.3 us (89%)
  local copies, waits for them, and re-layouts  1.57 us (7%)
  between operations  0.66 us (3%)
    pallas_call x1, Pallas kernels, body(): pl.pallas_call(functools.partial(kernel, dims), out_shape=jax.ShapeDtypeS...  20.3 us
    unnamed x1, local copies, waits for them, and re-layouts  1.57 us

profile of v4, /device:TPU:0, one launch (start us, length us, event | category | flops | bytes accessed | tf_op | source)
XLA Modules:
  0.0 22.5 jit_solution(14079152222025022436)
XLA Ops:
  0.7 20.3 %whiten_cross_stack.1 = f32[32,1024]{1,0:T(8,128)} custom-call(f32[64,2,1024]{2,1,0:T(2,128)} %traces_hbm.1, s32[4,48]{1,0:T(4,128)} %needed_hbm.1, s32[2,8]{1,0:T(2,128)} %home_hbm.1, s32[2,16]{1,0:T(2,128)} %partner_hbm.1, s32[1]{0:T(128)S(6)} %copy.12.live_ref, bf16[4,256,256]{2,1,0:T(8,128)(2,1)} %constant.10.clone.fwd_even_hbm, ...), custom_call_target="tpu_custom_call" | custom-call | flops 2000000000 | bytes 4000000 | tf_op jit(solution)/shard_map/whiten_cross_stack/pallas_call | solution.py:358
  20.9 1.6 %copy.13 = f32[32,1024]{1,0:T(8,128)} copy(f32[32,1024]{1,0:T(8,128)} %whiten_cross_stack.1) | data formatting | bytes 262144

commit v5 on v3

--- a/solution.py
+++ b/solution.py
@@ -86,6 +86,7 @@
     needed_hbm,
     home_hbm,
     partner_hbm,
+    live_ref,
     fwd_even_hbm,
     fwd_odd_hbm,
     band_hbm,
@@ -178,7 +179,20 @@
     choose = jnp.concatenate(choose, axis=0).astype(jnp.bfloat16)
 
     loads[0].wait()
-    rows = jnp.concatenate([traces[:, w, :] for w in range(win_dev)], axis=0)
+    tiles = samples // 128
+    rows = jnp.concatenate(
+        [
+            jnp.concatenate(
+                [
+                    traces[pl.ds(t * win_dev + w, chan_dev, stride=tiles * win_dev), :]
+                    for t in range(tiles)
+                ],
+                axis=1,
+            )
+            for w in range(win_dev)
+        ],
+        axis=0,
+    )
     count = rows.shape[0]
     folded = rows[:, :half] + rows[:, half:]
     odd_in = rows[:, :half] - rows[:, half:]
@@ -208,7 +222,7 @@
     )
     members = jnp.minimum(bins + BAND_REACH, half - 1) - jnp.maximum(bins - BAND_REACH, 0) + 1
     smooth = (both[:count] + both[count:]) * (1.0 / members.astype(jnp.float32))
-    factor = 1.0 / jnp.sqrt(smooth + 1e-05)
+    factor = lax.rsqrt(smooth + 1e-05)
 
     pl.semaphore_wait(barrier, len(greeted))
 
@@ -283,7 +297,9 @@
                     row = (b * homes + i) * partners + j
                     owner, inner = row // share_rows, row % share_rows
                     terms[h, owner, inner : inner + piece, :] = term[j : j + piece]
-        terms_out[h] = terms[h].astype(jnp.bfloat16)
+                    terms_out[h, owner, inner : inner + piece, :] = term[j : j + piece].astype(
+                        jnp.bfloat16
+                    )
         copies = []
         for n, (d, s) in enumerate(term_peers):
             copies.append(
@@ -301,6 +317,9 @@
 
     loads[4].wait()
     loads[5].wait()
+    for copies in list_copies:
+        for copy in copies:
+            copy.wait_send()
     parts = [None] * 4
     for h in range(2):
         total = [terms[h, win], None]
@@ -315,15 +334,16 @@
             table = inv_even[h] if k < 2 else inv_odd[h]
             both = dot(jnp.concatenate(halves(value), axis=0), table)
             parts[k] = both[:pad_rows] + both[pad_rows:]
+    for copies in term_copies:
+        for copy in copies:
+            copy.wait_send()
     even = jnp.concatenate([parts[0] + parts[1], parts[0] - parts[1]], axis=1)
     odd = parts[2] + parts[3]
     norm = 1.0 / math.sqrt(samples * win_dev * win_count)
+    row = win * share_rows + lax.broadcasted_iota(jnp.int32, (pad_rows, 1), 0)
+    norm = jnp.where(row < live_ref[0] * (homes * partners), norm, 0.0)
     out_ref[:, :half] = ((even - odd) * norm)[:share_rows]
     out_ref[:, half:] = ((even + odd) * norm)[:share_rows]
-
-    for copies in list_copies + term_copies:
-        for copy in copies:
-            copy.wait_send()
 
 
 def body(traces, needed, home_slot, partner_slot, live_blocks):
@@ -339,19 +359,22 @@
     quarter = samples // 4
     fwd_even, fwd_odd, band, inv_even, inv_odd = tables(samples)
     dims = (groups, win_count, chan_dev, win_dev, samples, listing, cap, cap_rows, blocks, homes, partners)
+    tiled = traces.reshape(chan_dev, win_dev, samples // 128, 128).transpose(0, 2, 1, 3)
+    tiled = tiled.reshape(-1, 128)
     vmem = pl.BlockSpec(memory_space=pltpu.VMEM)
+    smem = pl.BlockSpec(memory_space=pltpu.SMEM)
     hbm = pl.BlockSpec(memory_space=pltpu.HBM)
     bf16, f32 = jnp.bfloat16, jnp.float32
-    stacked = pl.pallas_call(
+    return pl.pallas_call(
         functools.partial(kernel, dims),
         out_shape=jax.ShapeDtypeStruct((share_rows, samples), f32),
-        in_specs=[hbm] * 9,
+        in_specs=[hbm] * 4 + [smem] + [hbm] * 5,
         out_specs=vmem,
         scratch_shapes=[
             pltpu.VMEM(needed.shape, jnp.int32),
             pltpu.VMEM(home_slot.shape, jnp.int32),
             pltpu.VMEM(partner_slot.shape, jnp.int32),
-            pltpu.VMEM(traces.shape, f32),
+            pltpu.VMEM(tiled.shape, f32),
             pltpu.VMEM(fwd_even.shape, bf16),
             pltpu.VMEM(fwd_odd.shape, bf16),
             pltpu.VMEM(band.shape, bf16),
@@ -376,18 +399,17 @@
         ),
         name="whiten_cross_stack",
     )(
-        traces,
+        tiled,
         needed,
         home_slot,
         partner_slot,
+        live_blocks,
         jnp.asarray(fwd_even),
         jnp.asarray(fwd_odd),
         jnp.asarray(band),
         jnp.asarray(inv_even),
         jnp.asarray(inv_odd),
     )
-    row = lax.axis_index("win") * share_rows + lax.broadcasted_iota(jnp.int32, (share_rows, 1), 0)
-    return stacked * (row // (homes * partners) < live_blocks[0]).astype(f32)
 
 
 def solution(mesh):

time: 23 us -> 22.3 us (0.970)
  other arithmetic: 2.16 us -> 0 us
  local copies, waits for them, and re-layouts: 0 us -> 1.57 us
    mul x1 -> x0, other arithmetic: 1.64 us -> none  [body(): return stacked * (row // (homes * partners) < live_blocks[0]).astype(f32)]
    unnamed x0 -> x1, local copies, waits for them, and re-layouts: none -> 1.57 us
    convert_element_type x1 -> x0, other arithmetic: 0.52 us -> none  [body(): return stacked * (row // (homes * partners) < live_blocks[0]).astype(f32)]
where the time goes in v5:
time: 22.3 us; the launch traced here: 22.2 us
  Pallas kernels  19.9 us (89%)
  local copies, waits for them, and re-layouts  1.57 us (7%)
  between operations  0.66 us (3%)
    pallas_call x1, Pallas kernels, body(): pl.pallas_call(functools.partial(kernel, dims), out_shape=jax.ShapeDtypeS...  19.9 us
    unnamed x1, local copies, waits for them, and re-layouts  1.57 us

profile of v5, /device:TPU:0, one launch (start us, length us, event | category | flops | bytes accessed | tf_op | source)
XLA Modules:
  0.0 22.2 jit_solution(8691093956683653214)
XLA Ops:
  0.7 19.9 %whiten_cross_stack.1 = f32[32,1024]{1,0:T(8,128)} custom-call(f32[1024,128]{1,0:T(8,128)} %bitcast.5, s32[4,48]{1,0:T(4,128)} %needed_hbm.1, s32[2,8]{1,0:T(2,128)} %home_hbm.1, s32[2,16]{1,0:T(2,128)} %partner_hbm.1, s32[1]{0:T(128)S(6)} %copy.13.live_ref, bf16[4,256,256]{2,1,0:T(8,128)(2,1)} %constant.10.clone.fwd_even_hbm, ...), custom_call_target="tpu_custom_call" | custom-call | flops 2000000000 | bytes 4000000 | tf_op jit(solution)/shard_map/whiten_cross_stack/pallas_call | solution.py:368
  20.6 1.6 %copy.14 = f32[32,1024]{1,0:T(8,128)} copy(f32[32,1024]{1,0:T(8,128)} %whiten_cross_stack.1) | data formatting | bytes 262144

commit v6 on v5

--- a/solution.py
+++ b/solution.py
@@ -104,20 +104,23 @@
     inv_odd,
     listed_out,
     listed_in,
-    terms,
-    terms_out,
-    terms_in,
+    last_in,
     load_sem,
     list_send,
     list_recv,
-    term_send,
-    term_recv,
+    fold_send,
+    fold_recv,
+    last_send,
+    last_recv,
+    *fold_refs,
 ):
     groups, win_count, chan_dev, win_dev, samples, listing, cap, cap_rows, blocks, homes, partners = dims
     chips = win_count // 2
     pairs = blocks * homes * partners
     share_rows = pairs // win_count
-    pad_rows = terms.shape[2]
+    rounds = chips.bit_length() - 1
+    sums, sums_out, fold_in = fold_refs[:rounds], fold_refs[rounds : 2 * rounds], fold_refs[2 * rounds :]
+    pad_rows = last_in.shape[2]
     quarter, half, eighth = samples // 4, samples // 2, samples // 8
     group = lax.axis_index("chan")
     win = lax.axis_index("win")
@@ -145,16 +148,18 @@
     barrier = pltpu.get_barrier_semaphore()
     cores = (core, 1 - core)
     list_peers = [(d, s) for s in range(2) for d in range(groups) if d or s]
-    term_peers = [(d, s) for d in reversed(range(chips)) for s in range(2) if d or s]
+    bits = [(chip // 2**t) % 2 for t in range(rounds)]
+    partner_chips = [chip + 2**t * (1 - 2 * bits[t]) for t in range(rounds)]
+    place_of = [int(format(z, f"0{rounds}b")[::-1], 2) for z in range(chips)]
 
     def list_id(d, s):
         return {"chan": lax.rem(group + d, groups), "win": chip * 2 + cores[s]}
 
-    def term_index(d, s):
-        return lax.rem(chip + d, chips) * 2 + cores[s]
+    def chip_id(t, s):
+        return {"win": partner_chips[t] * 2 + cores[s]}
 
     greeted = [list_id(d, s) for d, s in list_peers]
-    greeted += [{"win": term_index(d, s)} for d, s in term_peers if d]
+    greeted += [chip_id(t, 0) for t in range(rounds)] + [chip_id(rounds - 1, 1)]
     for peer in greeted:
         pl.semaphore_signal(barrier, inc=1, device_id=peer, device_id_type=MESH)
 
@@ -271,7 +276,43 @@
     wanted = jnp.concatenate([wanted + w * listing for w in range(win_dev)], axis=0)
     pick = jnp.where(wanted == code, 1.0, 0.0).astype(jnp.bfloat16)
 
-    term_copies = []
+    def fold_copy(h, t):
+        size = chips >> t + 1
+        return pltpu.make_async_remote_copy(
+            src_ref=sums_out[t].at[h, pl.ds((1 - bits[t]) * size, size)],
+            dst_ref=fold_in[t].at[h],
+            send_sem=fold_send.at[h, t],
+            recv_sem=fold_recv.at[h, t],
+            device_id=chip_id(t, 0),
+            device_id_type=MESH,
+        )
+
+    def last_copies(h):
+        bit, held = bits[-1], sums_out[-1]
+        plan = (
+            (held.at[h, 1 - bit, core], chip_id(rounds - 1, 0)),
+            (held.at[h, 1 - bit, 1 - core], chip_id(rounds - 1, 1)),
+            (held.at[h, bit, 1 - core], list_id(0, 1)),
+        )
+        return [
+            pltpu.make_async_remote_copy(
+                src_ref=src,
+                dst_ref=last_in.at[h, n],
+                send_sem=last_send.at[h, n],
+                recv_sem=last_recv.at[h, n],
+                device_id=peer,
+                device_id_type=MESH,
+            )
+            for n, (src, peer) in enumerate(plan)
+        ]
+
+    copies_of = {(h, t): [fold_copy(h, t)] for h in range(2) for t in range(rounds - 1)}
+    copies_of |= {(h, rounds - 1): last_copies(h) for h in range(2)}
+
+    def start(h, t):
+        for copy in copies_of[h, t]:
+            copy.start()
+
     piece = min(partners, share_rows)
     for h in range(2):
         for copy in list_copies[h]:
@@ -296,24 +337,19 @@
                 for j in range(0, partners, piece):
                     row = (b * homes + i) * partners + j
                     owner, inner = row // share_rows, row % share_rows
-                    terms[h, owner, inner : inner + piece, :] = term[j : j + piece]
-                    terms_out[h, owner, inner : inner + piece, :] = term[j : j + piece].astype(
-                        jnp.bfloat16
-                    )
-        copies = []
-        for n, (d, s) in enumerate(term_peers):
-            copies.append(
-                pltpu.make_async_remote_copy(
-                    src_ref=terms_out.at[h, term_index(d, s)],
-                    dst_ref=terms_in.at[h, n],
-                    send_sem=term_send.at[h, n],
-                    recv_sem=term_recv.at[h, n],
-                    device_id={"win": term_index(d, s)},
-                    device_id_type=MESH,
-                )
-            )
-            copies[-1].start()
-        term_copies.append(copies)
+                    at = (h, place_of[owner // 2], owner % 2, pl.ds(inner, piece))
+                    sums[0][at] = term[j : j + piece]
+                    sums_out[0][at] = term[j : j + piece].astype(jnp.bfloat16)
+        start(h, 0)
+
+    for t in range(rounds - 1):
+        size = chips >> t + 1
+        for h in range(2):
+            copies_of[h, t][0].wait_recv()
+            total = sums[t][h, pl.ds(bits[t] * size, size)] + fold_in[t][h].astype(jnp.float32)
+            sums[t + 1][h] = total
+            sums_out[t + 1][h] = total.astype(jnp.bfloat16)
+            start(h, t + 1)
 
     loads[4].wait()
     loads[5].wait()
@@ -322,11 +358,10 @@
             copy.wait_send()
     parts = [None] * 4
     for h in range(2):
-        total = [terms[h, win], None]
-        for n, (d, s) in enumerate(term_peers):
-            term_copies[h][n].wait_recv()
-            arrival = terms_in[h, n].astype(jnp.float32)
-            total[s] = arrival if total[s] is None else total[s] + arrival
+        for copy in copies_of[h, rounds - 1]:
+            copy.wait_recv()
+        got = [last_in[h, n].astype(jnp.float32) for n in range(3)]
+        total = [sums[-1][h, bits[-1], core] + got[0], got[1] + got[2]]
         for k, value in (
             (h, jnp.where(core == 0, total[0], total[1])),
             (2 + h, jnp.where(core == 0, total[1], total[0])),
@@ -334,7 +369,7 @@
             table = inv_even[h] if k < 2 else inv_odd[h]
             both = dot(jnp.concatenate(halves(value), axis=0), table)
             parts[k] = both[:pad_rows] + both[pad_rows:]
-    for copies in term_copies:
+    for copies in copies_of.values():
         for copy in copies:
             copy.wait_send()
     even = jnp.concatenate([parts[0] + parts[1], parts[0] - parts[1]], axis=1)
@@ -354,6 +389,8 @@
     cap_rows = -(-win_dev * cap // 16) * 16
     blocks, homes = home_slot.shape
     partners = partner_slot.shape[1]
+    chips = win_count // 2
+    rounds = chips.bit_length() - 1
     share_rows = blocks * homes * partners // win_count
     pad_rows = max(share_rows, 16)
     quarter = samples // 4
@@ -382,15 +419,18 @@
             pltpu.VMEM(inv_odd.shape, bf16),
             pltpu.VMEM((4, groups, cap_rows, quarter), bf16),
             pltpu.VMEM((2, 2, groups, cap_rows, quarter), bf16),
-            pltpu.VMEM((2, win_count, pad_rows, quarter), f32),
-            pltpu.VMEM((2, win_count, pad_rows, quarter), bf16),
-            pltpu.VMEM((2, win_count - 1, pad_rows, quarter), bf16),
+            pltpu.VMEM((2, 3, pad_rows, quarter), bf16),
             pltpu.SemaphoreType.DMA((9,)),
             pltpu.SemaphoreType.DMA((2, 2 * groups - 1)),
             pltpu.SemaphoreType.DMA((2, 2 * groups - 1)),
-            pltpu.SemaphoreType.DMA((2, win_count - 1)),
-            pltpu.SemaphoreType.DMA((2, win_count - 1)),
-        ],
+            pltpu.SemaphoreType.DMA((2, rounds)),
+            pltpu.SemaphoreType.DMA((2, rounds)),
+            pltpu.SemaphoreType.DMA((2, 3)),
+            pltpu.SemaphoreType.DMA((2, 3)),
+        ]
+        + [pltpu.VMEM((2, chips >> t, 2, pad_rows, quarter), f32) for t in range(rounds)]
+        + [pltpu.VMEM((2, chips >> t, 2, pad_rows, quarter), bf16) for t in range(rounds)]
+        + [pltpu.VMEM((2, chips >> t + 1, 2, pad_rows, quarter), bf16) for t in range(rounds - 1)],
         compiler_params=pltpu.CompilerParams(
             collective_id=0, has_side_effects=True, vmem_limit_bytes=64 * 1024 * 1024
         ),

time: 22.3 us -> 23.4 us (1.049)
  Pallas kernels: 19.9 us -> 21 us
    pallas_call x1, Pallas kernels: 19.9 us -> 21 us  [body(): pl.pallas_call(functools.partial(kernel, dims), out_shape=jax.ShapeDtypeS...]
where the time goes in v6:
time: 23.4 us; the launch traced here: 23.2 us
  Pallas kernels  21 us (90%)
  local copies, waits for them, and re-layouts  1.57 us (7%)
  between operations  0.66 us (3%)
    pallas_call x1, Pallas kernels, body(): pl.pallas_call(functools.partial(kernel, dims), out_shape=jax.ShapeDtypeS...  21 us
    unnamed x1, local copies, waits for them, and re-layouts  1.57 us

profile of v6, /device:TPU:0, one launch (start us, length us, event | category | flops | bytes accessed | tf_op | source)
XLA Modules:
  0.0 23.2 jit_solution(11482226148658414559)
XLA Ops:
  0.7 21.0 %whiten_cross_stack.1 = f32[32,1024]{1,0:T(8,128)} custom-call(f32[1024,128]{1,0:T(8,128)} %bitcast.5, s32[4,48]{1,0:T(4,128)} %needed_hbm.1, s32[2,8]{1,0:T(2,128)} %home_hbm.1, s32[2,16]{1,0:T(2,128)} %partner_hbm.1, s32[1]{0:T(128)S(6)} %copy.13.live_ref, bf16[4,256,256]{2,1,0:T(8,128)(2,1)} %constant.10.clone.fwd_even_hbm, ...), custom_call_target="tpu_custom_call" | custom-call | flops 2000000000 | bytes 4000000 | tf_op jit(solution)/shard_map/whiten_cross_stack/pallas_call | solution.py:405
  21.6 1.6 %copy.14 = f32[32,1024]{1,0:T(8,128)} copy(f32[32,1024]{1,0:T(8,128)} %whiten_cross_stack.1) | data formatting | bytes 262144

commit v7 on v5

--- a/solution.py
+++ b/solution.py
@@ -165,7 +165,7 @@
     first_mine = group * chan_dev
     place = lax.broadcasted_iota(jnp.int32, (listing, lanes), 0)
     out_row = lax.broadcasted_iota(jnp.int32, (cap_rows, lanes), 0)
-    for i in (6, 7, 8):
+    for i in (6, 7, 8, 0, 1, 2, 3):
         loads[i].wait()
     choose = []
     for d in range(groups):
@@ -178,7 +178,6 @@
         choose.append(jnp.where(out_row == target, 1.0, 0.0))
     choose = jnp.concatenate(choose, axis=0).astype(jnp.bfloat16)
 
-    loads[0].wait()
     tiles = samples // 128
     rows = jnp.concatenate(
         [
@@ -203,16 +202,13 @@
         both = dot(jnp.concatenate([high, low], axis=0), high_table)
         return both[:count] + both[count:] + dot(high, low_table)
 
-    loads[1].wait()
     spectra = [
         transform(even_in[0], fwd_even[0], fwd_even[1]),
         transform(even_in[1], fwd_even[2], fwd_even[3]),
     ]
-    loads[2].wait()
     odd_out = transform(odd_in, fwd_odd[0], fwd_odd[1])
     spectra += [odd_out[:, :quarter], odd_out[:, quarter:]]
     power = jnp.concatenate([s[:, :eighth] ** 2 + s[:, eighth:] ** 2 for s in spectra], axis=1)
-    loads[3].wait()
     both = dot(jnp.concatenate(halves(power), axis=0), band[...])
     spot = lax.broadcasted_iota(jnp.int32, (1, half), 1)
     bins = jnp.where(
@@ -223,8 +219,6 @@
     members = jnp.minimum(bins + BAND_REACH, half - 1) - jnp.maximum(bins - BAND_REACH, 0) + 1
     smooth = (both[:count] + both[count:]) * (1.0 / members.astype(jnp.float32))
     factor = lax.rsqrt(smooth + 1e-05)
-
-    pl.semaphore_wait(barrier, len(greeted))
 
     list_copies = []
     for h in range(2):
@@ -236,6 +230,8 @@
             chosen = dot(choose, whitened).astype(jnp.bfloat16)
             for d in range(groups):
                 listed_out[k, d] = chosen[d * cap_rows : (d + 1) * cap_rows]
+        if h == 0:
+            pl.semaphore_wait(barrier, len(greeted))
         copies = []
         for n, (d, s) in enumerate(list_peers):
             copies.append(

time: 22.3 us -> 22.5 us (level)
  no operation moved by 1% of the time
where the time goes in v7:
time: 22.5 us; the launch traced here: 22.4 us
  Pallas kernels  20.1 us (89%)
  local copies, waits for them, and re-layouts  1.57 us (7%)
  between operations  0.66 us (3%)
    pallas_call x1, Pallas kernels, body(): pl.pallas_call(functools.partial(kernel, dims), out_shape=jax.ShapeDtypeS...  20.1 us
    unnamed x1, local copies, waits for them, and re-layouts  1.57 us

profile of v7, /device:TPU:0, one launch (start us, length us, event | category | flops | bytes accessed | tf_op | source)
XLA Modules:
  0.0 22.4 jit_solution(10912147736215997780)
XLA Ops:
  0.7 20.1 %whiten_cross_stack.1 = f32[32,1024]{1,0:T(8,128)} custom-call(f32[1024,128]{1,0:T(8,128)} %bitcast.5, s32[4,48]{1,0:T(4,128)} %needed_hbm.1, s32[2,8]{1,0:T(2,128)} %home_hbm.1, s32[2,16]{1,0:T(2,128)} %partner_hbm.1, s32[1]{0:T(128)S(6)} %copy.13.live_ref, bf16[4,256,256]{2,1,0:T(8,128)(2,1)} %constant.10.clone.fwd_even_hbm, ...), custom_call_target="tpu_custom_call" | custom-call | flops 2000000000 | bytes 4000000 | tf_op jit(solution)/shard_map/whiten_cross_stack/pallas_call | solution.py:364
  20.8 1.6 %copy.14 = f32[32,1024]{1,0:T(8,128)} copy(f32[32,1024]{1,0:T(8,128)} %whiten_cross_stack.1) | data formatting | bytes 262144

commit v8 on v5

--- a/solution.py
+++ b/solution.py
@@ -45,9 +45,6 @@
     )
     fwd_even = np.stack([x for t in (fwd_a, fwd_b) for x in split_table(t)])
     fwd_odd = np.stack(split_table(fwd_o))
-    order = np.concatenate([bins_a, bins_b, bins_o])
-    inside = np.abs(order[:, None] - order[None, :]) <= BAND_REACH
-    band = inside.astype(np.float32).astype(ml_dtypes.bfloat16)
     inv_cos, inv_sin = inverse(half, bins_o)
     inv_even = np.stack(
         [
@@ -61,7 +58,7 @@
             for rows in (slice(0, eighth), slice(eighth, None))
         ]
     )
-    return fwd_even, fwd_odd, band, inv_even, inv_odd
+    return fwd_even, fwd_odd, inv_even, inv_odd
 
 
 def dot(left, right):
@@ -89,7 +86,6 @@
     live_ref,
     fwd_even_hbm,
     fwd_odd_hbm,
-    band_hbm,
     inv_even_hbm,
     inv_odd_hbm,
     out_ref,
@@ -99,7 +95,6 @@
     traces,
     fwd_even,
     fwd_odd,
-    band,
     inv_even,
     inv_odd,
     listed_out,
@@ -130,7 +125,6 @@
                 (traces_hbm, traces),
                 (fwd_even_hbm, fwd_even),
                 (fwd_odd_hbm, fwd_odd),
-                (band_hbm, band),
                 (inv_even_hbm, inv_even),
                 (inv_odd_hbm, inv_odd),
                 (needed_hbm, needed_ref),
@@ -139,7 +133,7 @@
             )
         )
     ]
-    for i in (6, 7, 8, 0, 1, 2, 3, 4, 5):
+    for i in (5, 0, 1, 2, 6, 7):
         loads[i].start()
 
     barrier = pltpu.get_barrier_semaphore()
@@ -157,6 +151,15 @@
     greeted += [{"win": term_index(d, s)} for d, s in term_peers if d]
     for peer in greeted:
         pl.semaphore_signal(barrier, inc=1, device_id=peer, device_id_type=MESH)
+
+    def bins_along(shape, axis):
+        spot = lax.broadcasted_iota(jnp.int32, shape, axis)
+        odd_or_b = jnp.where(spot < quarter, (spot - eighth) * 4 + 2, (spot - quarter) * 2 + 1)
+        return jnp.where(spot < eighth, spot * 4, odd_or_b)
+
+    bins = bins_along((1, half), 1)
+    apart = jnp.abs(bins_along((half, 1), 0) - bins)
+    band = jnp.where(apart <= BAND_REACH, 1.0, 0.0).astype(jnp.bfloat16)
 
     lanes = win_dev * chan_dev
     lane = lax.broadcasted_iota(jnp.int32, (1, lanes), 1)
@@ -165,8 +168,7 @@
     first_mine = group * chan_dev
     place = lax.broadcasted_iota(jnp.int32, (listing, lanes), 0)
     out_row = lax.broadcasted_iota(jnp.int32, (cap_rows, lanes), 0)
-    for i in (6, 7, 8):
-        loads[i].wait()
+    loads[5].wait()
     choose = []
     for d in range(groups):
         owner = lax.rem(group + d, groups)
@@ -212,14 +214,7 @@
     odd_out = transform(odd_in, fwd_odd[0], fwd_odd[1])
     spectra += [odd_out[:, :quarter], odd_out[:, quarter:]]
     power = jnp.concatenate([s[:, :eighth] ** 2 + s[:, eighth:] ** 2 for s in spectra], axis=1)
-    loads[3].wait()
-    both = dot(jnp.concatenate(halves(power), axis=0), band[...])
-    spot = lax.broadcasted_iota(jnp.int32, (1, half), 1)
-    bins = jnp.where(
-        spot < eighth,
-        spot * 4,
-        jnp.where(spot < quarter, (spot - eighth) * 4 + 2, (spot - quarter) * 2 + 1),
-    )
+    both = dot(jnp.concatenate(halves(power), axis=0), band)
     members = jnp.minimum(bins + BAND_REACH, half - 1) - jnp.maximum(bins - BAND_REACH, 0) + 1
     smooth = (both[:count] + both[count:]) * (1.0 / members.astype(jnp.float32))
     factor = lax.rsqrt(smooth + 1e-05)
@@ -251,6 +246,10 @@
             copies[-1].start()
         list_copies.append(copies)
         listed_in[h, 0, 0] = listed_out[core * 2 + h, 0]
+    for i in (3, 4):
+        loads[i].start()
+    for i in (6, 7):
+        loads[i].wait()
 
     mine = needed_ref[pl.ds(group, 1), :]
     arrived = lax.broadcasted_iota(jnp.int32, (1, groups * cap_rows), 1)
@@ -315,8 +314,8 @@
             copies[-1].start()
         term_copies.append(copies)
 
+    loads[3].wait()
     loads[4].wait()
-    loads[5].wait()
     for copies in list_copies:
         for copy in copies:
             copy.wait_send()
@@ -357,7 +356,7 @@
     share_rows = blocks * homes * partners // win_count
     pad_rows = max(share_rows, 16)
     quarter = samples // 4
-    fwd_even, fwd_odd, band, inv_even, inv_odd = tables(samples)
+    fwd_even, fwd_odd, inv_even, inv_odd = tables(samples)
     dims = (groups, win_count, chan_dev, win_dev, samples, listing, cap, cap_rows, blocks, homes, partners)
     tiled = traces.reshape(chan_dev, win_dev, samples // 128, 128).transpose(0, 2, 1, 3)
     tiled = tiled.reshape(-1, 128)
@@ -368,7 +367,7 @@
     return pl.pallas_call(
         functools.partial(kernel, dims),
         out_shape=jax.ShapeDtypeStruct((share_rows, samples), f32),
-        in_specs=[hbm] * 4 + [smem] + [hbm] * 5,
+        in_specs=[hbm] * 4 + [smem] + [hbm] * 4,
         out_specs=vmem,
         scratch_shapes=[
             pltpu.VMEM(needed.shape, jnp.int32),
@@ -377,7 +376,6 @@
             pltpu.VMEM(tiled.shape, f32),
             pltpu.VMEM(fwd_even.shape, bf16),
             pltpu.VMEM(fwd_odd.shape, bf16),
-            pltpu.VMEM(band.shape, bf16),
             pltpu.VMEM(inv_even.shape, bf16),
             pltpu.VMEM(inv_odd.shape, bf16),
             pltpu.VMEM((4, groups, cap_rows, quarter), bf16),
@@ -385,7 +383,7 @@
             pltpu.VMEM((2, win_count, pad_rows, quarter), f32),
             pltpu.VMEM((2, win_count, pad_rows, quarter), bf16),
             pltpu.VMEM((2, win_count - 1, pad_rows, quarter), bf16),
-            pltpu.SemaphoreType.DMA((9,)),
+            pltpu.SemaphoreType.DMA((8,)),
             pltpu.SemaphoreType.DMA((2, 2 * groups - 1)),
             pltpu.SemaphoreType.DMA((2, 2 * groups - 1)),
             pltpu.SemaphoreType.DMA((2, win_count - 1)),
@@ -406,7 +404,6 @@
         live_blocks,
         jnp.asarray(fwd_even),
         jnp.asarray(fwd_odd),
-        jnp.asarray(band),
         jnp.asarray(inv_even),
         jnp.asarray(inv_odd),
     )

time: 22.3 us -> 22.2 us (level)
  no operation moved by 1% of the time
where the time goes in v8:
time: 22.2 us; the launch traced here: 22 us
  Pallas kernels  19.8 us (89%)
  local copies, waits for them, and re-layouts  1.57 us (7%)
  between operations  0.66 us (3%)
    pallas_call x1, Pallas kernels, body(): pl.pallas_call(functools.partial(kernel, dims), out_shape=jax.ShapeDtypeS...  19.8 us
    unnamed x1, local copies, waits for them, and re-layouts  1.57 us

profile of v8, /device:TPU:0, one launch (start us, length us, event | category | flops | bytes accessed | tf_op | source)
XLA Modules:
  0.0 22.0 jit_solution(7953665253319232121)
XLA Ops:
  0.7 19.8 %whiten_cross_stack.1 = f32[32,1024]{1,0:T(8,128)} custom-call(f32[1024,128]{1,0:T(8,128)} %bitcast.5, s32[4,48]{1,0:T(4,128)} %needed_hbm.1, s32[2,8]{1,0:T(2,128)} %home_hbm.1, s32[2,16]{1,0:T(2,128)} %partner_hbm.1, s32[1]{0:T(128)S(6)} %copy.12.live_ref, bf16[4,256,256]{2,1,0:T(8,128)(2,1)} %constant.8.clone.fwd_even_hbm, ...), custom_call_target="tpu_custom_call" | custom-call | flops 2000000000 | bytes 4000000 | tf_op jit(solution)/shard_map/whiten_cross_stack/pallas_call | solution.py:367
  20.4 1.6 %copy.13 = f32[32,1024]{1,0:T(8,128)} copy(f32[32,1024]{1,0:T(8,128)} %whiten_cross_stack.1) | data formatting | bytes 262144

commit v9 on v8

--- a/solution.py
+++ b/solution.py
@@ -345,6 +345,17 @@
     out_ref[:, half:] = ((even + odd) * norm)[:share_rows]
 
 
+def hand_over(held, out, sems):
+    copies = [
+        pltpu.make_async_copy(held.at[pl.ds(at, 8)], out.at[pl.ds(at, 8)], sems.at[at // 8])
+        for at in range(0, held.shape[0], 8)
+    ]
+    for copy in copies:
+        copy.start()
+    for copy in copies:
+        copy.wait()
+
+
 def body(traces, needed, home_slot, partner_slot, live_blocks):
     chan_dev, win_dev, samples = traces.shape
     groups, win_count = lax.axis_size("chan"), lax.axis_size("win")
@@ -364,7 +375,7 @@
     smem = pl.BlockSpec(memory_space=pltpu.SMEM)
     hbm = pl.BlockSpec(memory_space=pltpu.HBM)
     bf16, f32 = jnp.bfloat16, jnp.float32
-    return pl.pallas_call(
+    stacked = pl.pallas_call(
         functools.partial(kernel, dims),
         out_shape=jax.ShapeDtypeStruct((share_rows, samples), f32),
         in_specs=[hbm] * 4 + [smem] + [hbm] * 4,
@@ -407,6 +418,15 @@
         jnp.asarray(inv_even),
         jnp.asarray(inv_odd),
     )
+    return pl.pallas_call(
+        hand_over,
+        out_shape=jax.ShapeDtypeStruct(stacked.shape, f32),
+        in_specs=[hbm],
+        out_specs=hbm,
+        scratch_shapes=[pltpu.SemaphoreType.DMA((share_rows // 8,))],
+        compiler_params=pltpu.CompilerParams(vmem_limit_bytes=64 * 1024 * 1024),
+        name="hand_over",
+    )(stacked)
 
 
 def solution(mesh):

time: 22.2 us -> 25.7 us (1.16)
  Pallas kernels: 19.8 us -> 24.9 us
  local copies, waits for them, and re-layouts: 1.57 us -> 0 us
    pallas_call x0 -> x1, Pallas kernels: none -> 5.11 us  [body(): pl.pallas_call(hand_over, out_shape=jax.ShapeDtypeStruct(stacked.shape, f...]
    unnamed x1 -> x0, local copies, waits for them, and re-layouts: 1.57 us -> none
where the time goes in v9:
time: 25.7 us; the launch traced here: 25.5 us
  Pallas kernels  24.9 us (97%)
  between operations  0.66 us (3%)
    pallas_call x1, Pallas kernels, body(): pl.pallas_call(functools.partial(kernel, dims), out_shape=jax.ShapeDtypeS...  19.8 us
    pallas_call x1, Pallas kernels, body(): pl.pallas_call(hand_over, out_shape=jax.ShapeDtypeStruct(stacked.shape, f...  5.11 us

profile of v9, /device:TPU:0, one launch (start us, length us, event | category | flops | bytes accessed | tf_op | source)
XLA Modules:
  0.0 25.5 jit_solution(249890892506401736)
XLA Ops:
  0.7 19.8 %whiten_cross_stack.1.held = f32[32,1024]{1,0:T(8,128)} custom-call(f32[1024,128]{1,0:T(8,128)} %bitcast.5, s32[4,48]{1,0:T(4,128)} %needed_hbm.1, s32[2,8]{1,0:T(2,128)} %home_hbm.1, s32[2,16]{1,0:T(2,128)} %partner_hbm.1, s32[1]{0:T(128)S(6)} %copy.11.live_ref, bf16[4,256,256]{2,1,0:T(8,128)(2,1)} %constant.8.clone.fwd_even_hbm, ...), custom_call_target="tpu_custom_call" | custom-call | flops 2000000000 | bytes 4000000 | tf_op jit(solution)/shard_map/whiten_cross_stack/pallas_call | solution.py:378
  20.4 5.1 %hand_over.1 = f32[32,1024]{1,0:T(8,128)} custom-call(f32[32,1024]{1,0:T(8,128)} %whiten_cross_stack.1.held), custom_call_target="tpu_custom_call" | custom-call | tf_op jit(solution)/shard_map/hand_over/pallas_call | solution.py:421

commit v10 on v8

--- a/solution.py
+++ b/solution.py
@@ -138,14 +138,22 @@
 
     barrier = pltpu.get_barrier_semaphore()
     cores = (core, 1 - core)
-    list_peers = [(d, s) for s in range(2) for d in range(groups) if d or s]
+
+    def flipped(place, d, count):
+        total = 0
+        for t in range(count.bit_length() - 1):
+            bit = (place // 2**t) % 2
+            total = total + (1 - bit if (d >> t) % 2 else bit) * 2**t
+        return total
+
+    list_peers = [(d, s) for d in reversed(range(groups)) for s in range(2) if d or s]
     term_peers = [(d, s) for d in reversed(range(chips)) for s in range(2) if d or s]
 
     def list_id(d, s):
-        return {"chan": lax.rem(group + d, groups), "win": chip * 2 + cores[s]}
+        return {"chan": flipped(group, d, groups), "win": chip * 2 + cores[s]}
 
     def term_index(d, s):
-        return lax.rem(chip + d, chips) * 2 + cores[s]
+        return flipped(chip, d, chips) * 2 + cores[s]
 
     greeted = [list_id(d, s) for d, s in list_peers]
     greeted += [{"win": term_index(d, s)} for d, s in term_peers if d]
@@ -171,7 +179,7 @@
     loads[5].wait()
     choose = []
     for d in range(groups):
-        owner = lax.rem(group + d, groups)
+        owner = flipped(group, d, groups)
         column = as_column(needed_ref[pl.ds(owner, 1), :])
         hit = column == (lane_chan + first_mine)
         found = jnp.sum(jnp.where(hit, place + 1, 0), axis=0, keepdims=True)
@@ -255,7 +263,7 @@
     arrived = lax.broadcasted_iota(jnp.int32, (1, groups * cap_rows), 1)
     code = jnp.full((1, groups * cap_rows), -1, jnp.int32)
     for d in range(groups):
-        source = lax.rem(group + groups - d, groups)
+        source = flipped(group, d, groups)
         begin = jnp.sum(
             (mine < source * chan_dev).astype(jnp.int32), axis=1, keepdims=True
         )

time: 22.2 us -> 22.3 us (level)
  no operation moved by 1% of the time
where the time goes in v10:
time: 22.3 us; the launch traced here: 22.1 us
  Pallas kernels  19.9 us (89%)
  local copies, waits for them, and re-layouts  1.57 us (7%)
  between operations  0.66 us (3%)
    pallas_call x1, Pallas kernels, body(): pl.pallas_call(functools.partial(kernel, dims), out_shape=jax.ShapeDtypeS...  19.9 us
    unnamed x1, local copies, waits for them, and re-layouts  1.57 us

profile of v10, /device:TPU:0, one launch (start us, length us, event | category | flops | bytes accessed | tf_op | source)
XLA Modules:
  0.0 22.1 jit_solution(3947684077406411429)
XLA Ops:
  0.7 19.9 %whiten_cross_stack.1 = f32[32,1024]{1,0:T(8,128)} custom-call(f32[1024,128]{1,0:T(8,128)} %bitcast.5, s32[4,48]{1,0:T(4,128)} %needed_hbm.1, s32[2,8]{1,0:T(2,128)} %home_hbm.1, s32[2,16]{1,0:T(2,128)} %partner_hbm.1, s32[1]{0:T(128)S(6)} %copy.12.live_ref, bf16[4,256,256]{2,1,0:T(8,128)(2,1)} %constant.8.clone.fwd_even_hbm, ...), custom_call_target="tpu_custom_call" | custom-call | flops 2000000000 | bytes 4000000 | tf_op jit(solution)/shard_map/whiten_cross_stack/pallas_call | solution.py:375
  20.6 1.6 %copy.13 = f32[32,1024]{1,0:T(8,128)} copy(f32[32,1024]{1,0:T(8,128)} %whiten_cross_stack.1) | data formatting | bytes 262144
